TPU v7x, 256 devices: a whole 4x4x8 slice. The times are simulated.
256 devices in a mesh: ctx: 128 (over x_lo, y, z, core), head: 2 (over x_hi).
Axes of the slice: x: 4 (x_hi: 2, x_lo: 2; x = x_hi * 2 + x_lo), y: 4, z: 8, core: 2. Of those that a mesh axis runs over, the one named last changes fastest.
Arguments:
- queries: bfloat16 [65536, 8, 4, 128], P('ctx', None, 'head'), may hold values from -6 to 6
- key_heads: bfloat16 [65536, 8, 128], P('ctx'), may hold values from -6 to 6
- value_heads: bfloat16 [65536, 8, 128], P('ctx'), may hold values from -6 to 6
- out_grad: bfloat16 [65536, 8, 4, 128], P('ctx', None, 'head'), may hold values from -6 to 6
- doc_ids: int32 [65536], P('ctx'), may hold values from 0 to 255, never falling along the last dimension, each value on 1 to 2048 neighbouring positions
Outputs:
- query_grad: bfloat16 [65536, 8, 4, 128], P('ctx', None, 'head')
- key_grad: bfloat16 [65536, 8, 128], P('ctx', 'head')
- value_grad: bfloat16 [65536, 8, 128], P('ctx', 'head')
Inputs may be any that keep to these rules, and one draw needn't show every extreme that they name: `doc_ids`: ids never fall along the sequence; a document has at most 2048 tokens.
All inputs are finite; a program needn't handle non-finite values.
Results may differ from a plain program's by a relative error of at most 0.012.
Values may be sent and summed in bfloat16 or wider, within the bound.
A program may use at most 64 MiB of HBM per device.

v0:
```python
import jax
import jax.numpy as jnp
from jax import lax
from jax.sharding import PartitionSpec as P

WINDOW = 256


def from_behind(block, axis, distance):
    devices = range(lax.axis_size(axis))
    route = [(i - distance, i) for i in devices if i - distance in devices]
    return lax.ppermute(block, axis, route)


def head_grads(query_n, key_n, value_n, grad_n, visible):
    scaling = 1.0 / query_n.shape[-1] ** 0.5
    scores = jnp.einsum("lgd,md->glm", query_n, key_n, preferred_element_type=jnp.float32) * scaling
    scores = jnp.where(visible[None], scores, -jnp.inf)
    top_score = jnp.max(scores, axis=-1, keepdims=True)
    weights = jnp.exp(scores - top_score)
    attn_prob = weights / jnp.sum(weights, axis=-1, keepdims=True)
    prob_low = attn_prob.astype(jnp.bfloat16)
    attended = jnp.einsum("glm,md->lgd", prob_low, value_n, preferred_element_type=jnp.float32)
    row_delta = jnp.sum(grad_n.astype(jnp.float32) * attended, axis=-1)
    grad_prob = jnp.einsum("lgd,md->glm", grad_n, value_n, preferred_element_type=jnp.float32)
    grad_low = (attn_prob * (grad_prob - jnp.transpose(row_delta)[:, :, None])).astype(jnp.bfloat16)
    query_part = (
        jnp.einsum("glm,md->lgd", grad_low, key_n, preferred_element_type=jnp.float32) * scaling
    ).astype(jnp.bfloat16)
    key_part = (
        jnp.einsum("glm,lgd->md", grad_low, query_n, preferred_element_type=jnp.float32) * scaling
    )
    value_part = jnp.einsum("glm,lgd->md", prob_low, grad_n, preferred_element_type=jnp.float32)
    return (query_part, key_part, value_part)


def visibility(doc_ids, prev_docs, block_rows, reach):
    anchor = lax.axis_index("ctx") * block_rows
    doc_key = jnp.concatenate([prev_docs, doc_ids], 0)
    pos_query = anchor + jnp.arange(block_rows, dtype=jnp.int32)
    pos_key = anchor - reach + jnp.arange(block_rows + reach, dtype=jnp.int32)
    lag_rows = pos_query[:, None] - pos_key[None, :]
    return (
        (lag_rows >= 0)
        & (lag_rows < reach)
        & (doc_ids[:, None] == doc_key[None, :])
        & (pos_key[None, :] >= 0)
    )


def run_heads(queries, out_grad, key_win, value_win, visible):
    window_rows = key_win.shape[0]
    kv_count = key_win.shape[1]
    head_size = key_win.shape[2]

    def head_step(kv_head, loop_state):
        query_acc, key_acc, value_acc = loop_state
        query_n = lax.dynamic_index_in_dim(queries, kv_head, 1, keepdims=False)
        grad_n = lax.dynamic_index_in_dim(out_grad, kv_head, 1, keepdims=False)
        key_n = lax.dynamic_index_in_dim(key_win, kv_head, 1, keepdims=False)
        value_n = lax.dynamic_index_in_dim(value_win, kv_head, 1, keepdims=False)
        query_part, key_part, value_part = head_grads(query_n, key_n, value_n, grad_n, visible)
        query_acc = lax.dynamic_update_index_in_dim(query_acc, query_part, kv_head, 1)
        key_acc = lax.dynamic_update_index_in_dim(key_acc, key_part, kv_head, 1)
        value_acc = lax.dynamic_update_index_in_dim(value_acc, value_part, kv_head, 1)
        return (query_acc, key_acc, value_acc)

    initial = (
        jnp.zeros_like(queries),
        jnp.zeros((window_rows, kv_count, head_size), jnp.float32),
        jnp.zeros((window_rows, kv_count, head_size), jnp.float32),
    )
    return lax.fori_loop(0, kv_count, head_step, initial)


def on_device(queries, key_heads, value_heads, out_grad, doc_ids):
    block_rows = queries.shape[0]
    reach = WINDOW
    tail_docs = doc_ids[block_rows - reach :]
    tail_keys = key_heads[block_rows - reach :]
    tail_values = value_heads[block_rows - reach :]
    prev_keys, prev_values, prev_docs = from_behind((tail_keys, tail_values, tail_docs), "ctx", 1)
    key_win = jnp.concatenate([prev_keys, key_heads], 0)
    value_win = jnp.concatenate([prev_values, value_heads], 0)
    visible = visibility(doc_ids, prev_docs, block_rows, reach)
    query_grad, key_acc, value_acc = run_heads(queries, out_grad, key_win, value_win, visible)
    back_keys, back_values = from_behind((key_acc[:reach], value_acc[:reach]), "ctx", -1)
    own_keys = key_acc[reach:].at[block_rows - reach :].add(back_keys)
    own_values = value_acc[reach:].at[block_rows - reach :].add(back_values)
    key_grad, value_grad = (
        lax.psum_scatter(own_keys, "head", scatter_dimension=1, tiled=True),
        lax.psum_scatter(own_values, "head", scatter_dimension=1, tiled=True),
    )
    return (query_grad, key_grad.astype(jnp.bfloat16), value_grad.astype(jnp.bfloat16))


def solution(mesh):
    in_specs = (
        P("ctx", None, "head", None),
        P("ctx", None, None),
        P("ctx", None, None),
        P("ctx", None, "head", None),
        P("ctx"),
    )
    out_specs = (P("ctx", None, "head", None), P("ctx", "head", None), P("ctx", "head", None))
    return jax.shard_map(
        on_device, mesh=mesh, in_specs=in_specs, out_specs=out_specs, check_vma=False
    )
```

profile of v0, /device:TPU:25, one launch (start us, length us, event | category | flops | bytes accessed | tf_op | source)
XLA Modules:
  0.0 295.8 jit_solution(14863334981653236929)
XLA Ops:
  9.5 4.1 %collective-permute-start = (bf16[256,8,128]{2,0,1:T(8,128)(2,1)}, bf16[256,8,128]{2,0,1:T(8,128)(2,1)}, u32[]{:S(2)}, u32[]{:S(2)}) collective-permute-start(bf16[256,8,128]{2,0,1:T(8,128)(2,1)} %slice.80), channel_id=1, source_target_pairs={{0,2},{2,4},{4,6},{6,8},{8,10},{10,12},{12,14},{14,16},{16,18},{18... | collective-permute-start | bytes 1572872 | tf_op jit(solution)/shard_map/ppermute | solution.py:12
  15.8 3.9 %collective-permute-start.2 = (bf16[256,8,128]{2,0,1:T(8,128)(2,1)S(1)}, bf16[256,8,128]{2,0,1:T(8,128)(2,1)S(1)}, u32[]{:S(2)}, u32[]{:S(2)}) collective-permute-start(bf16[256,8,128]{2,0,1:T(8,128)(2,1)S(1)} %slice.81), channel_id=1, source_target_pairs={{0,2},{2,4},{4,6},{6,8},{8,10},{10,12},{12,14},{14,16},{16,18},{18... | collective-permute-start | bytes 1572872 | tf_op jit(solution)/shard_map/ppermute | solution.py:12
  22.4 3.4 %collective-permute-done.2 = bf16[256,8,128]{2,0,1:T(8,128)(2,1)S(1)} collective-permute-done((bf16[256,8,128]{2,0,1:T(8,128)(2,1)S(1)}, bf16[256,8,128]{2,0,1:T(8,128)(2,1)S(1)}, u32[]{:S(2)}, u32[]{:S(2)}) %collective-permute-start.2) | collective-permute-done | bytes 524320 | tf_op jit(solution)/shard_map/ppermute | solution.py:12
  27.1 151.3 %while.20 = (s32[]{:T(128)}, bf16[512,8,2,128]{3,2,1,0:T(2,128)(2,1)}, f32[768,8,128]{2,0,1:T(8,128)}, f32[768,8,128]{2,0,1:T(8,128)}, bf16[768,8,128]{2,0,1:T(8...) while((s32[]{:T(128)}, ...), condition=%wide.region_4.5_spmd.clone, body=%wide.region_0.4_spmd.clone.sunk | while | flops 1219329792 | bytes 41712696 | solution.py:73
  29.3 4.1 %fusion.81 = (f32[2,512]{1,0:T(2,128)S(1)}, f32[2,512,768]{1,2,0:T(8,128)}) fusion(pred[512,768]{0,1:T(8,128)(4,1)S(1)} %fusion.80, bf16[512,1,2,128]{3,2,1,0:T(2,128)(2,1)S(1)} %get-tuple-element.364, bf16[768,8,128]{2,0,1:T(8,128)(2,1)} %get-tuple-element.400, s32[]{:T(128)S(6)} %copy.87), kind=kOutput, calls=%fused_computation.62.clone.1 | convolution fusion | flops 204473088 | bytes 4001796 | tf_op jit(solution)/shard_map/while/body/eval_jaxpr/sub | solution.py:20
  33.4 2.5 fusion.82
  48.2 4.1 %fusion.81 = (f32[2,512]{1,0:T(2,128)S(1)}, f32[2,512,768]{1,2,0:T(8,128)}) fusion(pred[512,768]{0,1:T(8,128)(4,1)S(1)} %fusion.80, bf16[512,1,2,128]{3,2,1,0:T(2,128)(2,1)S(1)} %get-tuple-element.364, bf16[768,8,128]{2,0,1:T(8,128)(2,1)} %get-tuple-element.400, s32[]{:T(128)S(6)} %copy.87), kind=kOutput, calls=%fused_computation.62.clone.1 | convolution fusion | flops 204473088 | bytes 4001796 | tf_op jit(solution)/shard_map/while/body/eval_jaxpr/sub | solution.py:20
  52.3 2.5 fusion.82
  60.3 2.3 fusion.86
  67.1 4.1 %fusion.81 = (f32[2,512]{1,0:T(2,128)S(1)}, f32[2,512,768]{1,2,0:T(8,128)}) fusion(pred[512,768]{0,1:T(8,128)(4,1)S(1)} %fusion.80, bf16[512,1,2,128]{3,2,1,0:T(2,128)(2,1)S(1)} %get-tuple-element.364, bf16[768,8,128]{2,0,1:T(8,128)(2,1)} %get-tuple-element.400, s32[]{:T(128)S(6)} %copy.87), kind=kOutput, calls=%fused_computation.62.clone.1 | convolution fusion | flops 204473088 | bytes 4001796 | tf_op jit(solution)/shard_map/while/body/eval_jaxpr/sub | solution.py:20
  71.2 2.5 fusion.82
  79.2 2.4 fusion.86
  86.0 4.1 %fusion.81 = (f32[2,512]{1,0:T(2,128)S(1)}, f32[2,512,768]{1,2,0:T(8,128)}) fusion(pred[512,768]{0,1:T(8,128)(4,1)S(1)} %fusion.80, bf16[512,1,2,128]{3,2,1,0:T(2,128)(2,1)S(1)} %get-tuple-element.364, bf16[768,8,128]{2,0,1:T(8,128)(2,1)} %get-tuple-element.400, s32[]{:T(128)S(6)} %copy.87), kind=kOutput, calls=%fused_computation.62.clone.1 | convolution fusion | flops 204473088 | bytes 4001796 | tf_op jit(solution)/shard_map/while/body/eval_jaxpr/sub | solution.py:20
  90.1 2.5 fusion.82
  98.1 2.4 fusion.86
  104.9 4.1 %fusion.81 = (f32[2,512]{1,0:T(2,128)S(1)}, f32[2,512,768]{1,2,0:T(8,128)}) fusion(pred[512,768]{0,1:T(8,128)(4,1)S(1)} %fusion.80, bf16[512,1,2,128]{3,2,1,0:T(2,128)(2,1)S(1)} %get-tuple-element.364, bf16[768,8,128]{2,0,1:T(8,128)(2,1)} %get-tuple-element.400, s32[]{:T(128)S(6)} %copy.87), kind=kOutput, calls=%fused_computation.62.clone.1 | convolution fusion | flops 204473088 | bytes 4001796 | tf_op jit(solution)/shard_map/while/body/eval_jaxpr/sub | solution.py:20
  109.0 2.5 fusion.82
  117.0 2.3 fusion.86
  123.8 4.1 %fusion.81 = (f32[2,512]{1,0:T(2,128)S(1)}, f32[2,512,768]{1,2,0:T(8,128)}) fusion(pred[512,768]{0,1:T(8,128)(4,1)S(1)} %fusion.80, bf16[512,1,2,128]{3,2,1,0:T(2,128)(2,1)S(1)} %get-tuple-element.364, bf16[768,8,128]{2,0,1:T(8,128)(2,1)} %get-tuple-element.400, s32[]{:T(128)S(6)} %copy.87), kind=kOutput, calls=%fused_computation.62.clone.1 | convolution fusion | flops 204473088 | bytes 4001796 | tf_op jit(solution)/shard_map/while/body/eval_jaxpr/sub | solution.py:20
  127.9 2.5 fusion.82
  136.0 2.4 fusion.86
  142.8 4.1 %fusion.81 = (f32[2,512]{1,0:T(2,128)S(1)}, f32[2,512,768]{1,2,0:T(8,128)}) fusion(pred[512,768]{0,1:T(8,128)(4,1)S(1)} %fusion.80, bf16[512,1,2,128]{3,2,1,0:T(2,128)(2,1)S(1)} %get-tuple-element.364, bf16[768,8,128]{2,0,1:T(8,128)(2,1)} %get-tuple-element.400, s32[]{:T(128)S(6)} %copy.87), kind=kOutput, calls=%fused_computation.62.clone.1 | convolution fusion | flops 204473088 | bytes 4001796 | tf_op jit(solution)/shard_map/while/body/eval_jaxpr/sub | solution.py:20
  146.9 2.5 fusion.82
  154.9 2.3 fusion.86
  161.7 4.1 %fusion.81 = (f32[2,512]{1,0:T(2,128)S(1)}, f32[2,512,768]{1,2,0:T(8,128)}) fusion(pred[512,768]{0,1:T(8,128)(4,1)S(1)} %fusion.80, bf16[512,1,2,128]{3,2,1,0:T(2,128)(2,1)S(1)} %get-tuple-element.364, bf16[768,8,128]{2,0,1:T(8,128)(2,1)} %get-tuple-element.400, s32[]{:T(128)S(6)} %copy.87), kind=kOutput, calls=%fused_computation.62.clone.1 | convolution fusion | flops 204473088 | bytes 4001796 | tf_op jit(solution)/shard_map/while/body/eval_jaxpr/sub | solution.py:20
  165.8 2.5 fusion.82
  179.7 6.4 %collective-permute-start.4 = (f32[256,8,128]{2,0,1:T(8,128)S(1)}, f32[256,8,128]{2,0,1:T(8,128)S(1)}, u32[]{:S(2)}, u32[]{:S(2)}) collective-permute-start(f32[256,8,128]{2,0,1:T(8,128)S(1)} %slice.79), channel_id=1, source_target_pairs={{2,0},{4,2},{6,4},{8,6},{10,8},{12,10},{14,12},{16,14},{18,16},{20... | collective-permute-start | bytes 3145736 | tf_op jit(solution)/shard_map/ppermute | solution.py:12
  187.8 8.8 %collective-permute-done.4 = f32[256,8,128]{2,0,1:T(8,128)S(1)} collective-permute-done((f32[256,8,128]{2,0,1:T(8,128)S(1)}, f32[256,8,128]{2,0,1:T(8,128)S(1)}, u32[]{:S(2)}, u32[]{:S(2)}) %collective-permute-start.4) | collective-permute-done | bytes 1048608 | tf_op jit(solution)/shard_map/ppermute | solution.py:12
  200.6 3.7 %collective-permute-start.3 = (f32[256,8,128]{2,0,1:T(8,128)S(1)}, f32[256,8,128]{2,0,1:T(8,128)S(1)}, u32[]{:S(2)}, u32[]{:S(2)}) collective-permute-start(f32[256,8,128]{2,0,1:T(8,128)S(1)} %slice.76), channel_id=1, source_target_pairs={{2,0},{4,2},{6,4},{8,6},{10,8},{12,10},{14,12},{16,14},{18,16},{20... | collective-permute-start | bytes 3145736 | tf_op jit(solution)/shard_map/ppermute | solution.py:12
  206.1 10.6 %collective-permute-done.3 = f32[256,8,128]{2,0,1:T(8,128)S(1)} collective-permute-done((f32[256,8,128]{2,0,1:T(8,128)S(1)}, f32[256,8,128]{2,0,1:T(8,128)S(1)}, u32[]{:S(2)}, u32[]{:S(2)}) %collective-permute-start.3) | collective-permute-done | bytes 1048608 | tf_op jit(solution)/shard_map/ppermute | solution.py:12
  219.5 20.8 %reduce-scatter.5.cloned.1.call-done = f32[512,4,128]{2,0,1:T(8,128)} async-done(((f32[512,8,128]{2,0,1:T(8,128)}), f32[512,4,128]{2,0,1:T(8,128)}) %reduce-scatter.5.cloned.1.call-update) | async-done | bytes 1048592 | tf_op jit(solution)/shard_map/reduce_scatter | solution.py:92
  242.8 43.6 %reduce-scatter.3.cloned.1.call-done = f32[512,4,128]{2,0,1:T(8,128)} async-done(((f32[512,8,128]{2,0,1:T(8,128)}), f32[512,4,128]{2,0,1:T(8,128)}) %reduce-scatter.3.cloned.1.call-update) | async-done | bytes 1048592 | tf_op jit(solution)/shard_map/reduce_scatter | solution.py:91
  (185 shorter events, 108.9 us)
Async XLA Ops:
  7.2 6.4 %copy-start.8 = (s32[512]{0:T(512)S(1)}, s32[512]{0:T(512)}, u32[]{:S(2)}) copy-start(s32[512]{0:T(512)} %param.15) | copy-start | bytes 6148
  7.2 8.4 %copy-start.7 = (bf16[512,8,128]{2,1,0:T(8,128)(2,1)S(1)}, bf16[512,8,128]{2,1,0:T(8,128)(2,1)}, u32[]{:S(2)}) copy-start(bf16[512,8,128]{2,1,0:T(8,128)(2,1)} %param.13) | copy-start | bytes 3145732
  7.2 233.1 %reduce-scatter.5.cloned.1.call-start = ((), (), s32[]{:S(2)}) async-start(), calls=%async_computation.3 | async-start | bytes 3145728 | tf_op jit(solution)/shard_map/reduce_scatter | solution.py:92
  9.5 10.5 %collective-permute-start = (bf16[256,8,128]{2,0,1:T(8,128)(2,1)}, bf16[256,8,128]{2,0,1:T(8,128)(2,1)}, u32[]{:S(2)}, u32[]{:S(2)}) collective-permute-start(bf16[256,8,128]{2,0,1:T(8,128)(2,1)} %slice.80), channel_id=1, source_target_pairs={{0,2},{2,4},{4,6},{6,8},{8,10},{10,12},{12,14},{14,16},{16,18},{18... | collective-permute-start | bytes 1572872 | tf_op jit(solution)/shard_map/ppermute | solution.py:12
  13.6 6.4 %collective-permute-start.1 = (s32[256]{0:T(256)S(1)}, s32[256]{0:T(256)S(1)}, u32[]{:S(2)}, u32[]{:S(2)}) collective-permute-start(s32[256]{0:T(256)S(1)} %slice.72), channel_id=1, source_target_pairs={{0,2},{2,4},{4,6},{6,8},{8,10},{10,12},{12,14},{14,16},{16,18},{18... | collective-permute-start | bytes 3080 | tf_op jit(solution)/shard_map/ppermute | solution.py:12
  15.8 10.0 %collective-permute-start.2 = (bf16[256,8,128]{2,0,1:T(8,128)(2,1)S(1)}, bf16[256,8,128]{2,0,1:T(8,128)(2,1)S(1)}, u32[]{:S(2)}, u32[]{:S(2)}) collective-permute-start(bf16[256,8,128]{2,0,1:T(8,128)(2,1)S(1)} %slice.81), channel_id=1, source_target_pairs={{0,2},{2,4},{4,6},{6,8},{8,10},{10,12},{12,14},{14,16},{16,18},{18... | collective-permute-start | bytes 1572872 | tf_op jit(solution)/shard_map/ppermute | solution.py:12
  29.3 4.1 %copy-start.3 = (bf16[512,1,2,128]{3,2,1,0:T(2,128)(2,1)}, bf16[512,1,2,128]{3,2,1,0:T(2,128)(2,1)S(1)}, u32[]{:S(2)}) copy-start(bf16[512,1,2,128]{3,2,1,0:T(2,128)(2,1)S(1)} %get-tuple-element.364) | copy-start | bytes 786436 | tf_op jit(solution)/shard_map/while
  29.3 8.4 %copy-start.1 = (bf16[512,1,2,128]{3,2,1,0:T(2,128)(2,1)}, bf16[512,1,2,128]{3,2,1,0:T(2,128)(2,1)S(1)}, u32[]{:S(2)}) copy-start(bf16[512,1,2,128]{3,2,1,0:T(2,128)(2,1)S(1)} %get-tuple-element.367) | copy-start | bytes 786436 | tf_op jit(solution)/shard_map/while
  33.4 4.3 %copy-start = (f32[2,512,768]{1,2,0:T(8,128)S(1)}, f32[2,512,768]{1,2,0:T(8,128)}, u32[]{:S(2)}) copy-start(f32[2,512,768]{1,2,0:T(8,128)} %get-tuple-element.365) | copy-start | bytes 9437188 | tf_op jit(solution)/shard_map/while
  48.2 4.1 %copy-start.3 = (bf16[512,1,2,128]{3,2,1,0:T(2,128)(2,1)}, bf16[512,1,2,128]{3,2,1,0:T(2,128)(2,1)S(1)}, u32[]{:S(2)}) copy-start(bf16[512,1,2,128]{3,2,1,0:T(2,128)(2,1)S(1)} %get-tuple-element.364) | copy-start | bytes 786436 | tf_op jit(solution)/shard_map/while
  48.2 8.4 %copy-start.1 = (bf16[512,1,2,128]{3,2,1,0:T(2,128)(2,1)}, bf16[512,1,2,128]{3,2,1,0:T(2,128)(2,1)S(1)}, u32[]{:S(2)}) copy-start(bf16[512,1,2,128]{3,2,1,0:T(2,128)(2,1)S(1)} %get-tuple-element.367) | copy-start | bytes 786436 | tf_op jit(solution)/shard_map/while
  52.3 4.3 %copy-start = (f32[2,512,768]{1,2,0:T(8,128)S(1)}, f32[2,512,768]{1,2,0:T(8,128)}, u32[]{:S(2)}) copy-start(f32[2,512,768]{1,2,0:T(8,128)} %get-tuple-element.365) | copy-start | bytes 9437188 | tf_op jit(solution)/shard_map/while
  67.1 4.1 %copy-start.3 = (bf16[512,1,2,128]{3,2,1,0:T(2,128)(2,1)}, bf16[512,1,2,128]{3,2,1,0:T(2,128)(2,1)S(1)}, u32[]{:S(2)}) copy-start(bf16[512,1,2,128]{3,2,1,0:T(2,128)(2,1)S(1)} %get-tuple-element.364) | copy-start | bytes 786436 | tf_op jit(solution)/shard_map/while
  67.1 8.4 %copy-start.1 = (bf16[512,1,2,128]{3,2,1,0:T(2,128)(2,1)}, bf16[512,1,2,128]{3,2,1,0:T(2,128)(2,1)S(1)}, u32[]{:S(2)}) copy-start(bf16[512,1,2,128]{3,2,1,0:T(2,128)(2,1)S(1)} %get-tuple-element.367) | copy-start | bytes 786436 | tf_op jit(solution)/shard_map/while
  71.2 4.3 %copy-start = (f32[2,512,768]{1,2,0:T(8,128)S(1)}, f32[2,512,768]{1,2,0:T(8,128)}, u32[]{:S(2)}) copy-start(f32[2,512,768]{1,2,0:T(8,128)} %get-tuple-element.365) | copy-start | bytes 9437188 | tf_op jit(solution)/shard_map/while
  86.0 4.1 %copy-start.3 = (bf16[512,1,2,128]{3,2,1,0:T(2,128)(2,1)}, bf16[512,1,2,128]{3,2,1,0:T(2,128)(2,1)S(1)}, u32[]{:S(2)}) copy-start(bf16[512,1,2,128]{3,2,1,0:T(2,128)(2,1)S(1)} %get-tuple-element.364) | copy-start | bytes 786436 | tf_op jit(solution)/shard_map/while
  86.0 8.4 %copy-start.1 = (bf16[512,1,2,128]{3,2,1,0:T(2,128)(2,1)}, bf16[512,1,2,128]{3,2,1,0:T(2,128)(2,1)S(1)}, u32[]{:S(2)}) copy-start(bf16[512,1,2,128]{3,2,1,0:T(2,128)(2,1)S(1)} %get-tuple-element.367) | copy-start | bytes 786436 | tf_op jit(solution)/shard_map/while
  90.1 4.3 %copy-start = (f32[2,512,768]{1,2,0:T(8,128)S(1)}, f32[2,512,768]{1,2,0:T(8,128)}, u32[]{:S(2)}) copy-start(f32[2,512,768]{1,2,0:T(8,128)} %get-tuple-element.365) | copy-start | bytes 9437188 | tf_op jit(solution)/shard_map/while
  104.9 4.1 %copy-start.3 = (bf16[512,1,2,128]{3,2,1,0:T(2,128)(2,1)}, bf16[512,1,2,128]{3,2,1,0:T(2,128)(2,1)S(1)}, u32[]{:S(2)}) copy-start(bf16[512,1,2,128]{3,2,1,0:T(2,128)(2,1)S(1)} %get-tuple-element.364) | copy-start | bytes 786436 | tf_op jit(solution)/shard_map/while
  104.9 8.4 %copy-start.1 = (bf16[512,1,2,128]{3,2,1,0:T(2,128)(2,1)}, bf16[512,1,2,128]{3,2,1,0:T(2,128)(2,1)S(1)}, u32[]{:S(2)}) copy-start(bf16[512,1,2,128]{3,2,1,0:T(2,128)(2,1)S(1)} %get-tuple-element.367) | copy-start | bytes 786436 | tf_op jit(solution)/shard_map/while
  109.0 4.3 %copy-start = (f32[2,512,768]{1,2,0:T(8,128)S(1)}, f32[2,512,768]{1,2,0:T(8,128)}, u32[]{:S(2)}) copy-start(f32[2,512,768]{1,2,0:T(8,128)} %get-tuple-element.365) | copy-start | bytes 9437188 | tf_op jit(solution)/shard_map/while
  123.8 8.4 %copy-start.1 = (bf16[512,1,2,128]{3,2,1,0:T(2,128)(2,1)}, bf16[512,1,2,128]{3,2,1,0:T(2,128)(2,1)S(1)}, u32[]{:S(2)}) copy-start(bf16[512,1,2,128]{3,2,1,0:T(2,128)(2,1)S(1)} %get-tuple-element.367) | copy-start | bytes 786436 | tf_op jit(solution)/shard_map/while
  127.9 4.3 %copy-start = (f32[2,512,768]{1,2,0:T(8,128)S(1)}, f32[2,512,768]{1,2,0:T(8,128)}, u32[]{:S(2)}) copy-start(f32[2,512,768]{1,2,0:T(8,128)} %get-tuple-element.365) | copy-start | bytes 9437188 | tf_op jit(solution)/shard_map/while
  142.7 4.1 %copy-start.3 = (bf16[512,1,2,128]{3,2,1,0:T(2,128)(2,1)}, bf16[512,1,2,128]{3,2,1,0:T(2,128)(2,1)S(1)}, u32[]{:S(2)}) copy-start(bf16[512,1,2,128]{3,2,1,0:T(2,128)(2,1)S(1)} %get-tuple-element.364) | copy-start | bytes 786436 | tf_op jit(solution)/shard_map/while
  142.8 8.4 %copy-start.1 = (bf16[512,1,2,128]{3,2,1,0:T(2,128)(2,1)}, bf16[512,1,2,128]{3,2,1,0:T(2,128)(2,1)S(1)}, u32[]{:S(2)}) copy-start(bf16[512,1,2,128]{3,2,1,0:T(2,128)(2,1)S(1)} %get-tuple-element.367) | copy-start | bytes 786436 | tf_op jit(solution)/shard_map/while
  146.9 4.3 %copy-start = (f32[2,512,768]{1,2,0:T(8,128)S(1)}, f32[2,512,768]{1,2,0:T(8,128)}, u32[]{:S(2)}) copy-start(f32[2,512,768]{1,2,0:T(8,128)} %get-tuple-element.365) | copy-start | bytes 9437188 | tf_op jit(solution)/shard_map/while
  161.7 4.1 %copy-start.3 = (bf16[512,1,2,128]{3,2,1,0:T(2,128)(2,1)}, bf16[512,1,2,128]{3,2,1,0:T(2,128)(2,1)S(1)}, u32[]{:S(2)}) copy-start(bf16[512,1,2,128]{3,2,1,0:T(2,128)(2,1)S(1)} %get-tuple-element.364) | copy-start | bytes 786436 | tf_op jit(solution)/shard_map/while
  161.7 8.4 %copy-start.1 = (bf16[512,1,2,128]{3,2,1,0:T(2,128)(2,1)}, bf16[512,1,2,128]{3,2,1,0:T(2,128)(2,1)S(1)}, u32[]{:S(2)}) copy-start(bf16[512,1,2,128]{3,2,1,0:T(2,128)(2,1)S(1)} %get-tuple-element.367) | copy-start | bytes 786436 | tf_op jit(solution)/shard_map/while
  165.8 4.3 %copy-start = (f32[2,512,768]{1,2,0:T(8,128)S(1)}, f32[2,512,768]{1,2,0:T(8,128)}, u32[]{:S(2)}) copy-start(f32[2,512,768]{1,2,0:T(8,128)} %get-tuple-element.365) | copy-start | bytes 9437188 | tf_op jit(solution)/shard_map/while
  179.7 16.9 %collective-permute-start.4 = (f32[256,8,128]{2,0,1:T(8,128)S(1)}, f32[256,8,128]{2,0,1:T(8,128)S(1)}, u32[]{:S(2)}, u32[]{:S(2)}) collective-permute-start(f32[256,8,128]{2,0,1:T(8,128)S(1)} %slice.79), channel_id=1, source_target_pairs={{2,0},{4,2},{6,4},{8,6},{10,8},{12,10},{14,12},{16,14},{18,16},{20... | collective-permute-start | bytes 3145736 | tf_op jit(solution)/shard_map/ppermute | solution.py:12
  199.3 87.2 %reduce-scatter.3.cloned.1.call-start = ((), (), s32[]{:S(2)}) async-start(), calls=%async_computation.2 | async-start | bytes 3145728 | tf_op jit(solution)/shard_map/reduce_scatter | solution.py:91
  200.6 16.1 %collective-permute-start.3 = (f32[256,8,128]{2,0,1:T(8,128)S(1)}, f32[256,8,128]{2,0,1:T(8,128)S(1)}, u32[]{:S(2)}, u32[]{:S(2)}) collective-permute-start(f32[256,8,128]{2,0,1:T(8,128)S(1)} %slice.76), channel_id=1, source_target_pairs={{2,0},{4,2},{6,4},{8,6},{10,8},{12,10},{14,12},{16,14},{18,16},{20... | collective-permute-start | bytes 3145736 | tf_op jit(solution)/shard_map/ppermute | solution.py:12
  (19 other events, 55.2 us)
Sparse Core Ops, SparseCore 0:
  199.4 40.8 reduce-scatter.4
  242.9 43.4 reduce-scatter.2
where the time goes:
time: 298 us; the launch traced here: 296 us
  matrix products  99.2 us (33%)
  waiting for transfers between devices  87.6 us (29%)
  local copies, waits for them, and re-layouts  39 us (13%)
  other arithmetic  35.1 us (12%)
  starting transfers between devices  20.1 us (7%)
  between operations  14.2 us (5%)
    reduce_scatter x1, waiting for transfers between devices, on_device(): lax.psum_scatter(own_keys, 'head', scatter_dimension=1, tiled=True)  43.6 us
    sub x8, matrix products, head_grads(): weights = jnp.exp(scores - top_score)  32.8 us
    ppermute x5, waiting for transfers between devices, from_behind(): return lax.ppermute(block, axis, route)  23.1 us
    reduce_scatter x1, waiting for transfers between devices, on_device(): lax.psum_scatter(own_values, 'head', scatter_dimension=1, tiled=True)  20.8 us
    ppermute x5, starting transfers between devices, from_behind(): return lax.ppermute(block, axis, route)  20 us
    convert_element_type x8, other arithmetic, head_grads(): prob_low = attn_prob.astype(jnp.bfloat16)  19.8 us
    dot_general x8, matrix products, head_grads(): jnp.einsum('glm,lgd->md', grad_low, query_n, preferred_element_type=jnp.f...  18.8 us
    dot_general x8, matrix products, head_grads(): jnp.einsum('glm,md->lgd', prob_low, value_n, preferred_element_type=jnp.f...  14.2 us
  transfers between devices with their start and end apart: 7, of which 6 were waited for; matrix products, arithmetic and copies ran while one was open for 4% of the time, Pallas kernels for 0%

commit v1 on v0

v1 whole, which is shorter than its diff:
```python
import functools

import jax
import jax.numpy as jnp
from jax import lax
from jax.experimental import pallas as pl
from jax.experimental.pallas import tpu as pltpu
from jax.sharding import PartitionSpec as P

MESH = pl.DeviceIdType.MESH
WINDOW = 256
TOK = 512
KV = 8
HD = 128
HALF = 4
NCTX = 128
SCALE = HD**-0.5
EXP_SCALE = SCALE * 1.4426950408889634
HIDDEN = -1e30
NT = (((1,), (1,)), ((), ()))
NN = (((1,), (0,)), ((), ()))
TN = (((0,), (0,)), ((), ()))
bf16 = jnp.bfloat16
f32 = jnp.float32


def dot(a, b, dims):
    return lax.dot_general(a, b, dims, preferred_element_type=f32)


def attention_tile(q, g, k, v, mask, onehot):
    s = dot(jnp.concatenate([k, mask], 1), jnp.concatenate([q, onehot], 1), NT)
    dp = dot(v, g, NT)
    top = jnp.max(s, 0, keepdims=True)
    e = jnp.exp2((s - top) * EXP_SCALE)
    total = jnp.sum(e, 0, keepdims=True)
    moment = jnp.sum(e * dp, 0, keepdims=True)
    inv = 1.0 / total
    p = e * inv
    ds = (p * (dp - moment * inv)).astype(bf16)
    p = p.astype(bf16)
    dv = dot(p, g, NN)
    dk = dot(ds, q, NN)
    dq_t = dot(k, ds, TN)
    return (dq_t * SCALE).T.astype(bf16), dk, dv


def kernel(
    q_hbm, k_hbm, v_hbm, g_hbm, doc_ref,
    dq_hbm, dk_hbm, dv_hbm,
    q_raw, g_raw, k_raw, v_raw, kt, vt, mask, onehot, doc_halo, doc_col,
    dq_s, ak, av, edge_s, edge_r, xs, xr, out_k, out_v,
    in_sem, kv_sem, f_send, f_recv, d_send, d_recv, e_send, e_recv, x_send, x_recv, dq_sem, out_sem,
):
    c = lax.axis_index("ctx")
    h = lax.axis_index("head")
    par = lax.rem(c, 2)
    first, last = c == 0, c == NCTX - 1
    has_prev, has_next = c > 0, c < NCTX - 1
    partner, nxt, prv = (c, 1 - h), (c + 1, h), (c - 1, h)

    def remote(src, dst, send, recv, dev):
        return pltpu.make_async_remote_copy(
            src_ref=src, dst_ref=dst, send_sem=send, recv_sem=recv, device_id=dev, device_id_type=MESH
        )

    def head_of(grp, i):
        return HALF * jnp.where(grp == 0, 1 - h, h) + i

    barrier = pltpu.get_barrier_semaphore()
    pl.semaphore_signal(barrier, inc=1, device_id=partner, device_id_type=MESH)

    @pl.when(has_prev)
    def _():
        pl.semaphore_signal(barrier, inc=1, device_id=prv, device_id_type=MESH)

    @pl.when(par == 0)
    def _():
        pl.semaphore_signal(barrier, inc=1, device_id=nxt, device_id_type=MESH)

    def kv_copy(j, r):
        src, dst = ((k_hbm, k_raw), (v_hbm, v_raw))[j]
        rows = pl.ds(r * WINDOW, WINDOW)
        return pltpu.make_async_copy(src.at[rows], dst.at[rows], kv_sem.at[j, r])

    def q_copy(n):
        return pltpu.make_async_copy(q_hbm.at[:, n], q_raw.at[n], in_sem.at[0, n])

    def g_copy(n):
        return pltpu.make_async_copy(g_hbm.at[:, n], g_raw.at[n], in_sem.at[1, n])

    for r in (1, 0):
        for j in (0, 1):
            kv_copy(j, r).start()

    def start_loads(i, _):
        n = head_of(i // HALF, lax.rem(i, HALF))
        q_copy(n).start()
        g_copy(n).start()
        return 0

    lax.fori_loop(0, KV, start_loads, 0)

    def clear(n, _):
        ak[n] = jnp.zeros((TOK + WINDOW, HD), f32)
        av[n] = jnp.zeros((TOK + WINDOW, HD), f32)
        return 0

    lax.fori_loop(0, KV, clear, 0)

    row = lax.broadcasted_iota(jnp.int32, (256, 128), 0)
    col = lax.broadcasted_iota(jnp.int32, (256, 128), 1)
    onehot[...] = jnp.where(row // 2 == col, 1.0, 0.0).astype(bf16)

    @pl.when(first)
    def _():
        kt[:, :WINDOW] = jnp.zeros((KV, WINDOW, HD), bf16)
        vt[:, :WINDOW] = jnp.zeros((KV, WINDOW, HD), bf16)
        doc_halo[...] = jnp.full((4, 128), -1, jnp.int32)

    @pl.when(last)
    def _():
        edge_r[...] = jnp.zeros(edge_r.shape, bf16)

    def swap(src, dst, r):
        def body(b, _):
            t = pl.multiple_of(r * WINDOW + b * 32, 32)
            dst[:, pl.ds(pl.multiple_of(t + WINDOW, 32), 32)] = jnp.swapaxes(src[pl.ds(t, 32)], 0, 1)
            return 0

        lax.fori_loop(0, WINDOW // 32, body, 0)

    for j, src, dst in ((0, k_raw, kt), (1, v_raw, vt)):
        kv_copy(j, 1).wait()
        swap(src, dst, 1)

    def doc_copy():
        return remote(doc_ref, doc_halo, d_send, d_recv, nxt)

    def halo_copy(n, j):
        ref = (kt, vt)[j]
        return remote(
            ref.at[n, pl.ds(TOK, WINDOW)], ref.at[n, pl.ds(0, WINDOW)], f_send.at[j, n], f_recv.at[j, n], nxt
        )

    @pl.when(par == 0)
    def _():
        pl.semaphore_wait(barrier, 2)

    @pl.when((par == 1) & has_next)
    def _():
        pl.semaphore_wait(barrier, 3)

    @pl.when(last)
    def _():
        pl.semaphore_wait(barrier, 2)

    @pl.when(has_next)
    def _():
        doc_copy().start()

        def send_halo(i, _):
            n = head_of(i // HALF, lax.rem(i, HALF))
            halo_copy(n, 0).start()
            halo_copy(n, 1).start()
            return 0

        lax.fori_loop(0, KV, send_halo, 0)

    for j, src, dst in ((0, k_raw, kt), (1, v_raw, vt)):
        kv_copy(j, 0).wait()
        swap(src, dst, 0)

    key_row = lax.broadcasted_iota(jnp.int32, (128, 128), 0)
    tok_col = lax.broadcasted_iota(jnp.int32, (128, 128), 1)

    def doc_columns(block, ref, r):
        wide = jnp.broadcast_to(ref[r : r + 1, :], (128, 128)).astype(f32)
        doc_col[block] = wide.T

    def build_mask(t):
        docs = jnp.broadcast_to(doc_ref[t : t + 1, :], (128, 128)).astype(f32)
        for b, inside in enumerate((key_row > tok_col, None, key_row <= tok_col)):
            same = doc_col[t + b] == docs
            seen = same if inside is None else same & inside
            mask[t, b * 128 : (b + 1) * 128] = jnp.where(seen, 0.0, HIDDEN).astype(bf16)

    for b in range(4):
        doc_columns(2 + b, doc_ref, b)
    build_mask(2)
    build_mask(3)

    def edge_copy(n, j):
        return remote(edge_s.at[n, j], edge_r.at[n, j], e_send.at[j, n], e_recv.at[j, n], prv)

    def x_copy(i, r, j):
        return remote(xs.at[i, r, j], xr.at[i, r, j], x_send.at[i, r, j], x_recv.at[i, r, j], partner)

    def dq_copy(n):
        return pltpu.make_async_copy(dq_s.at[n], dq_hbm.at[:, n], dq_sem.at[n])

    def send_tail_sums(i):
        n = head_of(0, i)

        @pl.when(has_next)
        def _():
            edge_copy(n, 0).wait_recv()
            edge_copy(n, 1).wait_recv()

        xs[i, 1, 0] = (ak[n, TOK:] * SCALE + edge_r[n, 0].astype(f32)).astype(bf16)
        xs[i, 1, 1] = (av[n, TOK:] + edge_r[n, 1].astype(f32)).astype(bf16)
        x_copy(i, 1, 0).start()
        x_copy(i, 1, 1).start()

    def step(s, _):
        i = lax.rem(s, HALF)
        late = lax.rem(s // HALF, 2)
        grp = s // (2 * HALF)
        n = head_of(grp, i)
        crossing = late + par == 1
        t0 = 2 * jnp.where(late == 1, par, 1 - par)

        @pl.when(late == 0)
        def _():
            q_copy(n).wait()
            g_copy(n).wait()

        @pl.when(crossing & (i == 0) & (grp == 0))
        def _():
            @pl.when(has_prev)
            def _():
                doc_copy().wait_recv()

            doc_columns(0, doc_halo, 2)
            doc_columns(1, doc_halo, 3)
            build_mask(0)
            build_mask(1)

        @pl.when(crossing & has_prev)
        def _():
            halo_copy(n, 0).wait_recv()
            halo_copy(n, 1).wait_recv()

        res = []
        for j in range(2):
            t = t0 + j
            rows = pl.ds(pl.multiple_of(t * 256, 256), 256)
            keys = pl.ds(pl.multiple_of(t * 128, 128), 384)
            q = q_raw.at[n].reshape(1024, 128)[rows, :]
            g = g_raw.at[n].reshape(1024, 128)[rows, :]
            dq, dk, dv = attention_tile(q, g, kt[n, keys], vt[n, keys], mask[t], onehot[...])
            dq_s.at[n].reshape(1024, 128)[rows, :] = dq
            res.append((dk, dv))
        base = pl.ds(pl.multiple_of(t0 * 128, 128), TOK)
        for acc, x, y in ((ak, res[0][0], res[1][0]), (av, res[0][1], res[1][1])):
            acc[n, base] += jnp.concatenate([x[:128], x[128:] + y[:256], y[256:]], 0)

        @pl.when(crossing & has_prev)
        def _():
            edge_s[n, 0] = (ak[n, :WINDOW] * SCALE).astype(bf16)
            edge_s[n, 1] = av[n, :WINDOW].astype(bf16)
            edge_copy(n, 0).start()
            edge_copy(n, 1).start()

        @pl.when(late == 1)
        def _():
            dq_copy(n).start()

        @pl.when((late == 1) & (grp == 0))
        def _():
            xs[i, 0, 0] = (ak[n, WINDOW:TOK] * SCALE).astype(bf16)
            xs[i, 0, 1] = av[n, WINDOW:TOK].astype(bf16)
            x_copy(i, 0, 0).start()
            x_copy(i, 0, 1).start()

        @pl.when((par == 0) & (s >= 1) & (s <= HALF))
        def _():
            send_tail_sums(s - 1)

        @pl.when((par == 1) & (s >= 2 * HALF) & (s < 3 * HALF))
        def _():
            send_tail_sums(s - 2 * HALF)

        return 0

    lax.fori_loop(0, 4 * HALF, step, 0)

    def out_copy(j, r):
        src, dst = ((out_k, dk_hbm), (out_v, dv_hbm))[j]
        rows = pl.ds(r * WINDOW, WINDOW)
        return pltpu.make_async_copy(src.at[rows], dst.at[rows], out_sem.at[j, r])

    def finish(r):
        def wait_head(i, _):
            x_copy(i, r, 0).wait_recv()
            x_copy(i, r, 1).wait_recv()
            if r == 1:

                @pl.when(has_next)
                def _():
                    edge_copy(HALF * h + i, 0).wait_recv()
                    edge_copy(HALF * h + i, 1).wait_recv()

            return 0

        lax.fori_loop(0, HALF, wait_head, 0)
        own = pl.ds(HALF * h, HALF)

        def body(b, _):
            t = pl.multiple_of(b * 32, 32)
            part = pl.ds(t, 32)
            accs = pl.ds(pl.multiple_of((r + 1) * WINDOW + t, 32), 32)
            outs = pl.ds(pl.multiple_of(r * WINDOW + t, 32), 32)
            for j, acc, scale, out in ((0, ak, SCALE, out_k), (1, av, None, out_v)):
                val = acc[own, accs]
                if scale is not None:
                    val = val * scale
                val = val + xr[:, r, j, part].astype(f32)
                if r == 1:
                    val = val + edge_r[own, j, part].astype(f32)
                out[outs] = jnp.swapaxes(val.astype(bf16), 0, 1)
            return 0

        lax.fori_loop(0, WINDOW // 32, body, 0)
        out_copy(0, r).start()
        out_copy(1, r).start()

    @pl.when(par == 0)
    def _():
        finish(1)
        finish(0)

    @pl.when(par == 1)
    def _():
        finish(0)
        finish(1)

    @pl.when(has_next)
    def _():
        doc_copy().wait_send()

    def drain(n, _):
        @pl.when(has_next)
        def _():
            halo_copy(n, 0).wait_send()
            halo_copy(n, 1).wait_send()

        @pl.when(has_prev)
        def _():
            edge_copy(n, 0).wait_send()
            edge_copy(n, 1).wait_send()

        dq_copy(n).wait()
        return 0

    lax.fori_loop(0, KV, drain, 0)

    def drain_x(i, _):
        for r in range(2):
            for j in range(2):
                x_copy(i, r, j).wait_send()
        return 0

    lax.fori_loop(0, HALF, drain_x, 0)
    for r in range(2):
        for j in range(2):
            out_copy(j, r).wait()


def on_device(queries, key_heads, value_heads, out_grad, doc_ids):
    hbm = pl.BlockSpec(memory_space=pl.ANY)
    vmem = pl.BlockSpec(memory_space=pltpu.VMEM)
    dma = pltpu.SemaphoreType.DMA
    return pl.pallas_call(
        kernel,
        out_shape=(
            jax.ShapeDtypeStruct((TOK, KV, 2, HD), bf16),
            jax.ShapeDtypeStruct((TOK, HALF, HD), bf16),
            jax.ShapeDtypeStruct((TOK, HALF, HD), bf16),
        ),
        in_specs=[hbm, hbm, hbm, hbm, vmem],
        out_specs=(hbm, hbm, hbm),
        scratch_shapes=[
            pltpu.VMEM((KV, TOK, 2, HD), bf16),
            pltpu.VMEM((KV, TOK, 2, HD), bf16),
            pltpu.VMEM((TOK, KV, HD), bf16),
            pltpu.VMEM((TOK, KV, HD), bf16),
            pltpu.VMEM((KV, TOK + WINDOW, HD), bf16),
            pltpu.VMEM((KV, TOK + WINDOW, HD), bf16),
            pltpu.VMEM((4, 384, HD), bf16),
            pltpu.VMEM((256, HD), bf16),
            pltpu.VMEM((4, 128), jnp.int32),
            pltpu.VMEM((6, 128, 128), f32),
            pltpu.VMEM((KV, TOK, 2, HD), bf16),
            pltpu.VMEM((KV, TOK + WINDOW, HD), f32),
            pltpu.VMEM((KV, TOK + WINDOW, HD), f32),
            pltpu.VMEM((KV, 2, WINDOW, HD), bf16),
            pltpu.VMEM((KV, 2, WINDOW, HD), bf16),
            pltpu.VMEM((HALF, 2, 2, WINDOW, HD), bf16),
            pltpu.VMEM((HALF, 2, 2, WINDOW, HD), bf16),
            pltpu.VMEM((TOK, HALF, HD), bf16),
            pltpu.VMEM((TOK, HALF, HD), bf16),
            dma((2, KV)),
            dma((2, 2)),
            dma((2, KV)),
            dma((2, KV)),
            dma(()),
            dma(()),
            dma((2, KV)),
            dma((2, KV)),
            dma((HALF, 2, 2)),
            dma((HALF, 2, 2)),
            dma((KV,)),
            dma((2, 2)),
        ],
        compiler_params=pltpu.CompilerParams(
            collective_id=0, has_side_effects=True, vmem_limit_bytes=56 * 1024 * 1024
        ),
        cost_estimate=pl.CostEstimate(flops=8 * 10**9, bytes_accessed=9 * 2**20, transcendentals=3 * 10**6),
    )(queries, key_heads, value_heads, out_grad, doc_ids.reshape(4, 128))


def solution(mesh):
    return jax.shard_map(
        on_device,
        mesh=mesh,
        in_specs=(
            P("ctx", None, "head", None),
            P("ctx", None, None),
            P("ctx", None, None),
            P("ctx", None, "head", None),
            P("ctx"),
        ),
        out_specs=(P("ctx", None, "head", None), P("ctx", "head", None), P("ctx", "head", None)),
        check_vma=False,
    )
```

time: 298 us -> 53.2 us (0.18)
  matrix products: 99.2 us -> 0 us
  waiting for transfers between devices: 87.6 us -> 0 us
  Pallas kernels: 0 us -> 46.4 us
  other arithmetic: 35.1 us -> 0 us
  local copies, waits for them, and re-layouts: 39 us -> 6.03 us
  starting transfers between devices: 20.1 us -> 0 us
  between operations: 14.2 us -> 0.66 us
    dot_general x40 -> x0, matrix products: 66.5 us -> none  [the longest x8 18.8 us: head_grads(): jnp.einsum('glm,lgd->md', grad_low, query_n, preferred_element_type=jnp.f...]
    reduce_scatter x2 -> x0, waiting for transfers between devices: 64.4 us -> none  [the longest x1 43.6 us: on_device(): lax.psum_scatter(own_keys, 'head', scatter_dimension=1, tiled=True)]
    pallas_call x0 -> x1, Pallas kernels: none -> 46.4 us  [on_device(): pl.pallas_call(kernel, out_shape=(jax.ShapeDtypeStruct((TOK, KV, 2, HD),...]
    sub x8 -> x0, matrix products: 32.8 us -> none  [head_grads(): weights = jnp.exp(scores - top_score)]
    ppermute x5 -> x0, waiting for transfers between devices: 23.1 us -> none  [from_behind(): return lax.ppermute(block, axis, route)]
    convert_element_type x10 -> x0, other arithmetic: 22.4 us -> none  [the longest x8 19.8 us: head_grads(): prob_low = attn_prob.astype(jnp.bfloat16)]
    ppermute x5 -> x0, starting transfers between devices: 20 us -> none  [from_behind(): return lax.ppermute(block, axis, route)]
    dynamic_update_slice x16 -> x0, local copies, waits for them, and re-layouts: 14 us -> none  [head_step(): lax.dynamic_update_index_in_dim(query_acc, query_part, kv_head, 1)]
  transfers between devices with their start and end apart: 7 -> 0, of which waited for: 6 -> 0; matrix products, arithmetic and copies ran while one was open for 4% -> 0% of each run, Pallas kernels for 0% -> 0%
where the time goes in v1:
time: 53.2 us; the launch traced here: 53.1 us
  Pallas kernels  46.4 us (87%)
  local copies, waits for them, and re-layouts  6.03 us (11%)
  between operations  0.66 us (1%)
    pallas_call x1, Pallas kernels, on_device(): pl.pallas_call(kernel, out_shape=(jax.ShapeDtypeStruct((TOK, KV, 2, HD),...  46.4 us
    unnamed x7, local copies, waits for them, and re-layouts  6.03 us

profile of v1, /device:TPU:25, one launch (start us, length us, event | category | flops | bytes accessed | tf_op | source)
XLA Modules:
  0.0 53.1 jit_solution(11922269554174200189)
XLA Ops:
  0.6 46.4 %shard_map.76 = (bf16[512,8,2,128]{3,2,1,0:T(2,128)(2,1)}, bf16[512,4,128]{2,1,0:T(4,128)(2,1)}, bf16[512,4,128]{2,1,0:T(4,128)(2,1)}) custom-call(bf16[512,8,2,128]{3,2,1,0:T(2,128)(2,1)} %q_hbm.1, bf16[512,8,128]{2,1,0:T(8,128)(2,1)} %k_hbm.1, bf16[512,8,128]{2,1,0:T(8,128)(2,1)} %v_hbm.1, bf16[512,8,2,128]{3,2,1,0:T(2,128)(2,1)} %g_hbm.1, s32[4,128]{1,0:T(4,128)} %bitcast.1), custom_call_target="tpu_custom_call" | custom-call | flops 8000000000 | bytes 9437184 | tf_op jit(solution)/shard_map/pallas_call | solution.py:374
  47.1 0.0 copy-start.1
  47.1 0.0 copy-start
  47.1 4.4 %copy.11 = bf16[512,8,2,128]{3,2,1,0:T(2,128)(2,1)} copy(bf16[512,8,2,128]{3,2,1,0:T(2,128)(2,1)} %get-tuple-element.6) | data formatting | bytes 4194304
  51.5 0.0 copy-done.1
  51.5 0.8 %copy.12 = bf16[512,4,128]{2,1,0:T(4,128)(2,1)} copy(bf16[512,4,128]{2,1,0:T(4,128)(2,1)S(1)} %copy-done.1) | data formatting | bytes 1048576
  52.3 0.0 copy-done
  52.3 0.8 %copy.13 = bf16[512,4,128]{2,1,0:T(4,128)(2,1)} copy(bf16[512,4,128]{2,1,0:T(4,128)(2,1)S(1)} %copy-done) | data formatting | bytes 1048576
Async XLA Ops:
  47.1 4.5 %copy-start.1 = (bf16[512,4,128]{2,1,0:T(4,128)(2,1)S(1)}, bf16[512,4,128]{2,1,0:T(4,128)(2,1)}, u32[]{:S(2)}) copy-start(bf16[512,4,128]{2,1,0:T(4,128)(2,1)} %get-tuple-element.7) | copy-start | bytes 1572868
  47.1 5.2 %copy-start = (bf16[512,4,128]{2,1,0:T(4,128)(2,1)S(1)}, bf16[512,4,128]{2,1,0:T(4,128)(2,1)}, u32[]{:S(2)}) copy-start(bf16[512,4,128]{2,1,0:T(4,128)(2,1)} %get-tuple-element.8) | copy-start | bytes 1572868

commit v2 on v1

--- a/solution.py
+++ b/solution.py
@@ -14,9 +14,11 @@
 HD = 128
 HALF = 4
 NCTX = 128
+TURN = NCTX // 2
 SCALE = HD**-0.5
 EXP_SCALE = SCALE * 1.4426950408889634
 HIDDEN = -1e30
+PIECES = 4
 NT = (((1,), (1,)), ((), ()))
 NN = (((1,), (0,)), ((), ()))
 TN = (((0,), (0,)), ((), ()))
@@ -57,7 +59,9 @@
     par = lax.rem(c, 2)
     first, last = c == 0, c == NCTX - 1
     has_prev, has_next = c > 0, c < NCTX - 1
+    before_turn, after_turn = c == TURN - 1, c == TURN
     partner, nxt, prv = (c, 1 - h), (c + 1, h), (c - 1, h)
+    nxt_v = (c + 1, jnp.where(before_turn, 1 - h, h))
 
     def remote(src, dst, send, recv, dev):
         return pltpu.make_async_remote_copy(
@@ -77,6 +81,10 @@
     @pl.when(par == 0)
     def _():
         pl.semaphore_signal(barrier, inc=1, device_id=nxt, device_id_type=MESH)
+
+    @pl.when(after_turn)
+    def _():
+        pl.semaphore_signal(barrier, inc=1, device_id=(c - 1, 1 - h), device_id_type=MESH)
 
     def kv_copy(j, r):
         src, dst = ((k_hbm, k_raw), (v_hbm, v_raw))[j]
@@ -139,17 +147,22 @@
 
     def halo_copy(n, j):
         ref = (kt, vt)[j]
+        dev = (nxt, nxt_v)[j]
         return remote(
-            ref.at[n, pl.ds(TOK, WINDOW)], ref.at[n, pl.ds(0, WINDOW)], f_send.at[j, n], f_recv.at[j, n], nxt
+            ref.at[n, pl.ds(TOK, WINDOW)], ref.at[n, pl.ds(0, WINDOW)], f_send.at[j, n], f_recv.at[j, n], dev
         )
 
     @pl.when(par == 0)
     def _():
         pl.semaphore_wait(barrier, 2)
 
-    @pl.when((par == 1) & has_next)
+    @pl.when((par == 1) & has_next & jnp.logical_not(before_turn))
     def _():
         pl.semaphore_wait(barrier, 3)
+
+    @pl.when(before_turn)
+    def _():
+        pl.semaphore_wait(barrier, 4)
 
     @pl.when(last)
     def _():
@@ -191,6 +204,12 @@
     build_mask(3)
 
     def edge_copy(n, j):
+        cross = after_turn & (n // HALF != h)
+        slot = jnp.where(cross, lax.rem(n + HALF, KV), n)
+        dev = (c - 1, jnp.where(cross, 1 - h, h))
+        return remote(edge_s.at[n, j], edge_r.at[slot, j], e_send.at[j, n], e_recv.at[j, slot], dev)
+
+    def edge_arrival(n, j):
         return remote(edge_s.at[n, j], edge_r.at[n, j], e_send.at[j, n], e_recv.at[j, n], prv)
 
     def x_copy(i, r, j):
@@ -202,13 +221,21 @@
     def send_tail_sums(i):
         n = head_of(0, i)
 
-        @pl.when(has_next)
-        def _():
-            edge_copy(n, 0).wait_recv()
-            edge_copy(n, 1).wait_recv()
-
-        xs[i, 1, 0] = (ak[n, TOK:] * SCALE + edge_r[n, 0].astype(f32)).astype(bf16)
-        xs[i, 1, 1] = (av[n, TOK:] + edge_r[n, 1].astype(f32)).astype(bf16)
+        @pl.when(before_turn)
+        def _():
+            xs[i, 1, 0] = (ak[n, TOK:] * SCALE).astype(bf16)
+            xs[i, 1, 1] = av[n, TOK:].astype(bf16)
+
+        @pl.when(jnp.logical_not(before_turn))
+        def _():
+            @pl.when(has_next)
+            def _():
+                edge_arrival(n, 0).wait_recv()
+                edge_arrival(n, 1).wait_recv()
+
+            xs[i, 1, 0] = (ak[n, TOK:] * SCALE + edge_r[n, 0].astype(f32)).astype(bf16)
+            xs[i, 1, 1] = (av[n, TOK:] + edge_r[n, 1].astype(f32)).astype(bf16)
+
         x_copy(i, 1, 0).start()
         x_copy(i, 1, 1).start()
 
@@ -298,8 +325,16 @@
 
                 @pl.when(has_next)
                 def _():
-                    edge_copy(HALF * h + i, 0).wait_recv()
-                    edge_copy(HALF * h + i, 1).wait_recv()
+                    edge_arrival(HALF * h + i, 0).wait_recv()
+                    edge_arrival(HALF * h + i, 1).wait_recv()
+
+                @pl.when(before_turn)
+                def _():
+                    n, slot = head_of(1, i), head_of(0, i)
+                    edge_arrival(slot, 0).wait_recv()
+                    edge_arrival(slot, 1).wait_recv()
+                    ak[n, TOK:] += edge_r[slot, 0].astype(f32) * (1.0 / SCALE)
+                    av[n, TOK:] += edge_r[slot, 1].astype(f32)
 
             return 0
 
@@ -367,11 +402,23 @@
             out_copy(j, r).wait()
 
 
+def deliver(dq_in, dk_in, dv_in, dq_out, dk_out, dv_out, sem):
+    copies = []
+    for j in range(PIECES):
+        rows = pl.ds(j * (TOK // PIECES), TOK // PIECES)
+        for a, (src, dst) in enumerate(((dq_in, dq_out), (dk_in, dk_out), (dv_in, dv_out))):
+            copies.append(pltpu.make_async_copy(src.at[rows], dst.at[rows], sem.at[a, j]))
+    for copy in copies:
+        copy.start()
+    for copy in copies:
+        copy.wait()
+
+
 def on_device(queries, key_heads, value_heads, out_grad, doc_ids):
     hbm = pl.BlockSpec(memory_space=pl.ANY)
     vmem = pl.BlockSpec(memory_space=pltpu.VMEM)
     dma = pltpu.SemaphoreType.DMA
-    return pl.pallas_call(
+    parts = pl.pallas_call(
         kernel,
         out_shape=(
             jax.ShapeDtypeStruct((TOK, KV, 2, HD), bf16),
@@ -418,6 +465,14 @@
         ),
         cost_estimate=pl.CostEstimate(flops=8 * 10**9, bytes_accessed=9 * 2**20, transcendentals=3 * 10**6),
     )(queries, key_heads, value_heads, out_grad, doc_ids.reshape(4, 128))
+    return pl.pallas_call(
+        deliver,
+        out_shape=tuple(jax.ShapeDtypeStruct(p.shape, p.dtype) for p in parts),
+        in_specs=[hbm] * 3,
+        out_specs=(hbm,) * 3,
+        scratch_shapes=[dma((3, PIECES))],
+        compiler_params=pltpu.CompilerParams(vmem_limit_bytes=56 * 1024 * 1024),
+    )(*parts)
 
 
 def solution(mesh):

time: 53.2 us -> 138 us (2.59)
  Pallas kernels: 46.4 us -> 137 us
  local copies, waits for them, and re-layouts: 6.03 us -> 0 us
    pallas_call x0 -> x1, Pallas kernels: none -> 96.5 us  [on_device(): pl.pallas_call(deliver, out_shape=tuple((jax.ShapeDtypeStruct(p.shape, p....]
    unnamed x7 -> x0, local copies, waits for them, and re-layouts: 6.03 us -> none
    pallas_call x1, Pallas kernels: 46.4 us -> 40.8 us  [on_device(): pl.pallas_call(kernel, out_shape=(jax.ShapeDtypeStruct((TOK, KV, 2, HD),...]
where the time goes in v2:
time: 138 us
  Pallas kernels  137 us (99%)
    pallas_call x1, Pallas kernels, on_device(): pl.pallas_call(deliver, out_shape=tuple((jax.ShapeDtypeStruct(p.shape, p....  96.5 us
    pallas_call x1, Pallas kernels, on_device(): pl.pallas_call(kernel, out_shape=(jax.ShapeDtypeStruct((TOK, KV, 2, HD),...  40.8 us

profile of v2, /device:TPU:25, one launch (start us, length us, event | category | flops | bytes accessed | tf_op | source)
XLA Modules:
  0.0 138.0 jit_solution(4417146713045997652)
XLA Ops:
  0.6 40.8 %shard_map.76 = (bf16[512,8,2,128]{3,2,1,0:T(2,128)(2,1)}, bf16[512,4,128]{2,1,0:T(4,128)(2,1)}, bf16[512,4,128]{2,1,0:T(4,128)(2,1)}) custom-call(bf16[512,8,2,128]{3,2,1,0:T(2,128)(2,1)} %q_hbm.1, bf16[512,8,128]{2,1,0:T(8,128)(2,1)} %k_hbm.1, bf16[512,8,128]{2,1,0:T(8,128)(2,1)} %v_hbm.1, bf16[512,8,2,128]{3,2,1,0:T(2,128)(2,1)} %g_hbm.1, s32[4,128]{1,0:T(4,128)} %bitcast.1), custom_call_target="tpu_custom_call" | custom-call | flops 8000000000 | bytes 9437184 | tf_op jit(solution)/shard_map/pallas_call | solution.py:421
  41.5 96.5 %shard_map.77 = (bf16[512,8,2,128]{3,2,1,0:T(2,128)(2,1)}, bf16[512,4,128]{2,1,0:T(4,128)(2,1)}, bf16[512,4,128]{2,1,0:T(4,128)(2,1)}) custom-call(bf16[512,8,2,128]{3,2,1,0:T(2,128)(2,1)} %get-tuple-element.6.dq_in, bf16[512,4,128]{2,1,0:T(4,128)(2,1)} %get-tuple-element.7.dk_in, bf16[512,4,128]{2,1,0:T(4,128)(2,1)} %get-tuple-element.8.dv_in), custom_call_target="tpu_custom_call" | custom-call | tf_op jit(solution)/shard_map/pallas_call | solution.py:468

commit v3 on v2

--- a/solution.py
+++ b/solution.py
@@ -19,6 +19,7 @@
 EXP_SCALE = SCALE * 1.4426950408889634
 HIDDEN = -1e30
 PIECES = 4
+CHUNK = 128
 NT = (((1,), (1,)), ((), ()))
 NN = (((1,), (0,)), ((), ()))
 TN = (((0,), (0,)), ((), ()))
@@ -30,28 +31,12 @@
     return lax.dot_general(a, b, dims, preferred_element_type=f32)
 
 
-def attention_tile(q, g, k, v, mask, onehot):
-    s = dot(jnp.concatenate([k, mask], 1), jnp.concatenate([q, onehot], 1), NT)
-    dp = dot(v, g, NT)
-    top = jnp.max(s, 0, keepdims=True)
-    e = jnp.exp2((s - top) * EXP_SCALE)
-    total = jnp.sum(e, 0, keepdims=True)
-    moment = jnp.sum(e * dp, 0, keepdims=True)
-    inv = 1.0 / total
-    p = e * inv
-    ds = (p * (dp - moment * inv)).astype(bf16)
-    p = p.astype(bf16)
-    dv = dot(p, g, NN)
-    dk = dot(ds, q, NN)
-    dq_t = dot(k, ds, TN)
-    return (dq_t * SCALE).T.astype(bf16), dk, dv
-
-
 def kernel(
     q_hbm, k_hbm, v_hbm, g_hbm, doc_ref,
     dq_hbm, dk_hbm, dv_hbm,
-    q_raw, g_raw, k_raw, v_raw, kt, vt, mask, onehot, doc_halo, doc_col,
-    dq_s, ak, av, edge_s, edge_r, xs, xr, out_k, out_v,
+    q_raw, g_raw, k_raw, v_raw, qt, gt, kt, vt, mask, onehot, doc_halo, doc_col,
+    dqt, dq_s, ak, av, edge_s, edge_r, xs, xr, out_k, out_v,
+    s_a, s_b, dp_a, dp_b, p_a, p_b, ds_a, ds_b,
     in_sem, kv_sem, f_send, f_recv, d_send, d_recv, e_send, e_recv, x_send, x_recv, dq_sem, out_sem,
 ):
     c = lax.axis_index("ctx")
@@ -91,23 +76,17 @@
         rows = pl.ds(r * WINDOW, WINDOW)
         return pltpu.make_async_copy(src.at[rows], dst.at[rows], kv_sem.at[j, r])
 
-    def q_copy(n):
-        return pltpu.make_async_copy(q_hbm.at[:, n], q_raw.at[n], in_sem.at[0, n])
-
-    def g_copy(n):
-        return pltpu.make_async_copy(g_hbm.at[:, n], g_raw.at[n], in_sem.at[1, n])
-
-    for r in (1, 0):
+    def qg_copy(j, part):
+        src, dst = ((q_hbm, q_raw), (g_hbm, g_raw))[j]
+        return pltpu.make_async_copy(src.at[:, part], dst.at[part], in_sem.at[j, part])
+
+    for j in (0, 1):
+        kv_copy(j, 1).start()
+    for j in (0, 1):
+        kv_copy(j, 0).start()
+    for part in (1 - h, h):
         for j in (0, 1):
-            kv_copy(j, r).start()
-
-    def start_loads(i, _):
-        n = head_of(i // HALF, lax.rem(i, HALF))
-        q_copy(n).start()
-        g_copy(n).start()
-        return 0
-
-    lax.fori_loop(0, KV, start_loads, 0)
+            qg_copy(j, part).start()
 
     def clear(n, _):
         ak[n] = jnp.zeros((TOK + WINDOW, HD), f32)
@@ -116,9 +95,12 @@
 
     lax.fori_loop(0, KV, clear, 0)
 
-    row = lax.broadcasted_iota(jnp.int32, (256, 128), 0)
-    col = lax.broadcasted_iota(jnp.int32, (256, 128), 1)
-    onehot[...] = jnp.where(row // 2 == col, 1.0, 0.0).astype(bf16)
+    key_row = lax.broadcasted_iota(jnp.int32, (128, 128), 0)
+    tok_col = lax.broadcasted_iota(jnp.int32, (128, 128), 1)
+    onehot[:128] = jnp.where(key_row == tok_col, 1.0, 0.0).astype(bf16)
+    onehot[128:] = jnp.where(key_row == tok_col, 1.0, 0.0).astype(bf16)
+    p_b[...] = jnp.zeros(p_b.shape, bf16)
+    ds_b[...] = jnp.zeros(ds_b.shape, bf16)
 
     @pl.when(first)
     def _():
@@ -132,11 +114,11 @@
 
     def swap(src, dst, r):
         def body(b, _):
-            t = pl.multiple_of(r * WINDOW + b * 32, 32)
-            dst[:, pl.ds(pl.multiple_of(t + WINDOW, 32), 32)] = jnp.swapaxes(src[pl.ds(t, 32)], 0, 1)
+            t = pl.multiple_of(r * WINDOW + b * CHUNK, CHUNK)
+            dst[:, pl.ds(pl.multiple_of(t + WINDOW, CHUNK), CHUNK)] = jnp.swapaxes(src[pl.ds(t, CHUNK)], 0, 1)
             return 0
 
-        lax.fori_loop(0, WINDOW // 32, body, 0)
+        lax.fori_loop(0, WINDOW // CHUNK, body, 0)
 
     for j, src, dst in ((0, k_raw, kt), (1, v_raw, vt)):
         kv_copy(j, 1).wait()
@@ -175,7 +157,7 @@
         def send_halo(i, _):
             n = head_of(i // HALF, lax.rem(i, HALF))
             halo_copy(n, 0).start()
-            halo_copy(n, 1).start()
+            halo_copy(jnp.where(before_turn, lax.rem(n + HALF, KV), n), 1).start()
             return 0
 
         lax.fori_loop(0, KV, send_halo, 0)
@@ -183,9 +165,6 @@
     for j, src, dst in ((0, k_raw, kt), (1, v_raw, vt)):
         kv_copy(j, 0).wait()
         swap(src, dst, 0)
-
-    key_row = lax.broadcasted_iota(jnp.int32, (128, 128), 0)
-    tok_col = lax.broadcasted_iota(jnp.int32, (128, 128), 1)
 
     def doc_columns(block, ref, r):
         wide = jnp.broadcast_to(ref[r : r + 1, :], (128, 128)).astype(f32)
@@ -215,8 +194,28 @@
     def x_copy(i, r, j):
         return remote(xs.at[i, r, j], xr.at[i, r, j], x_send.at[i, r, j], x_recv.at[i, r, j], partner)
 
-    def dq_copy(n):
-        return pltpu.make_async_copy(dq_s.at[n], dq_hbm.at[:, n], dq_sem.at[n])
+    def dq_copy(part):
+        return pltpu.make_async_copy(dq_s.at[part], dq_hbm.at[:, part], dq_sem.at[part])
+
+    def swap_in(part):
+        for j, src, dst in ((0, q_raw, qt), (1, g_raw, gt)):
+            qg_copy(j, part).wait()
+
+            def body(b, _, src=src, dst=dst):
+                t = pl.ds(pl.multiple_of(b * CHUNK, CHUNK), CHUNK)
+                dst[pl.ds(part * KV, KV), t] = jnp.swapaxes(src[part, t], 0, 1)
+                return 0
+
+            lax.fori_loop(0, TOK // CHUNK, body, 0)
+
+    def swap_out(part):
+        def body(b, _):
+            t = pl.ds(pl.multiple_of(b * CHUNK, CHUNK), CHUNK)
+            dq_s[part, t] = jnp.swapaxes(dqt[pl.ds(part * KV, KV), t], 0, 1)
+            return 0
+
+        lax.fori_loop(0, TOK // CHUNK, body, 0)
+        dq_copy(part).start()
 
     def send_tail_sums(i):
         n = head_of(0, i)
@@ -239,18 +238,25 @@
         x_copy(i, 1, 0).start()
         x_copy(i, 1, 1).start()
 
-    def step(s, _):
+    def plan(s):
         i = lax.rem(s, HALF)
-        late = lax.rem(s // HALF, 2)
         grp = s // (2 * HALF)
-        n = head_of(grp, i)
-        crossing = late + par == 1
+        late = lax.rem(s // HALF + jnp.where((grp == 1) & (par == 0), 1, 0), 2)
         t0 = 2 * jnp.where(late == 1, par, 1 - par)
-
-        @pl.when(late == 0)
-        def _():
-            q_copy(n).wait()
-            g_copy(n).wait()
+        return i, late, grp, head_of(grp, i), t0, late + par == 1
+
+    def places(n, t0, j):
+        t = t0 + j
+        toks = pl.ds(pl.multiple_of(t * 128, 128), 128)
+        keys = pl.ds(pl.multiple_of(t * 128, 128), 384)
+        return t, (pl.ds(2 * n, 2), toks), keys
+
+    def prepare(s):
+        i, _, grp, n, _, crossing = plan(s)
+
+        @pl.when(s == 2 * HALF)
+        def _():
+            swap_in(h)
 
         @pl.when(crossing & (i == 0) & (grp == 0))
         def _():
@@ -268,19 +274,50 @@
             halo_copy(n, 0).wait_recv()
             halo_copy(n, 1).wait_recv()
 
-        res = []
+    def front(s, s_to, dp_to):
+        _, _, _, n, t0, _ = plan(s)
         for j in range(2):
-            t = t0 + j
-            rows = pl.ds(pl.multiple_of(t * 256, 256), 256)
-            keys = pl.ds(pl.multiple_of(t * 128, 128), 384)
-            q = q_raw.at[n].reshape(1024, 128)[rows, :]
-            g = g_raw.at[n].reshape(1024, 128)[rows, :]
-            dq, dk, dv = attention_tile(q, g, kt[n, keys], vt[n, keys], mask[t], onehot[...])
-            dq_s.at[n].reshape(1024, 128)[rows, :] = dq
-            res.append((dk, dv))
-        base = pl.ds(pl.multiple_of(t0 * 128, 128), TOK)
-        for acc, x, y in ((ak, res[0][0], res[1][0]), (av, res[0][1], res[1][1])):
-            acc[n, base] += jnp.concatenate([x[:128], x[128:] + y[:256], y[256:]], 0)
+            t, where, keys = places(n, t0, j)
+            q = qt[where].reshape(256, HD)
+            s_to[j] = dot(jnp.concatenate([kt[n, keys], mask[t]], 1), jnp.concatenate([q, onehot[...]], 1), NT)
+            yield
+            dp_to[j] = dot(vt[n, keys], gt[where].reshape(256, HD), NT)
+            yield
+
+    def middle(s_of, dp_of, p_to, ds_to):
+        for j in range(2):
+            for part in (slice(0, 128), slice(128, 256)):
+                scores = s_of[j, :, part]
+                dp = dp_of[j, :, part]
+                top = jnp.max(scores, 0, keepdims=True)
+                e = jnp.exp2((scores - top) * EXP_SCALE)
+                total = jnp.sum(e, 0, keepdims=True)
+                moment = jnp.sum(e * dp, 0, keepdims=True)
+                inv = 1.0 / total
+                p = e * inv
+                ds_to[j, :, part] = (p * (dp - moment * inv)).astype(bf16)
+                p_to[j, :, part] = p.astype(bf16)
+                yield
+
+    def back(s, p_of, ds_of):
+        _, _, _, n, t0, _ = plan(s)
+        for j in range(2):
+            _, where, keys = places(n, t0, j)
+            ds = ds_of[j]
+            ak[n, keys] += dot(ds, qt[where].reshape(256, HD), NN)
+            av[n, keys] += dot(p_of[j], gt[where].reshape(256, HD), NN)
+            yield
+            dq = (dot(kt[n, keys], ds, TN) * SCALE).T.astype(bf16)
+            dqt[where] = dq.reshape(2, 128, HD)
+            yield
+
+    def weave(*works):
+        works = list(works)
+        while works:
+            works = [w for w in works if next(w, True) is None]
+
+    def pass_on(s):
+        i, late, grp, n, _, crossing = plan(s)
 
         @pl.when(crossing & has_prev)
         def _():
@@ -289,10 +326,6 @@
             edge_copy(n, 0).start()
             edge_copy(n, 1).start()
 
-        @pl.when(late == 1)
-        def _():
-            dq_copy(n).start()
-
         @pl.when((late == 1) & (grp == 0))
         def _():
             xs[i, 0, 0] = (ak[n, WINDOW:TOK] * SCALE).astype(bf16)
@@ -308,9 +341,41 @@
         def _():
             send_tail_sums(s - 2 * HALF)
 
+        @pl.when(s == 2 * HALF - 1)
+        def _():
+            swap_out(1 - h)
+
+    steps = 4 * HALF
+    slots = ((s_a, dp_a, p_a, ds_a), (s_b, dp_b, p_b, ds_b))
+    swap_in(1 - h)
+    prepare(0)
+    weave(front(0, s_a, dp_a))
+
+    def pair(at, _):
+        for k in range(2):
+            s = 2 * at + k
+            here, other = slots[k], slots[1 - k]
+
+            @pl.when(s + 1 < steps)
+            def _():
+                prepare(s + 1)
+
+            weave(
+                middle(*here),
+                back(jnp.maximum(s - 1, 0), other[2], other[3]),
+                front(jnp.minimum(s + 1, steps - 1), other[0], other[1]),
+            )
+
+            @pl.when(s >= 1)
+            def _():
+                pass_on(s - 1)
+
         return 0
 
-    lax.fori_loop(0, 4 * HALF, step, 0)
+    lax.fori_loop(0, steps // 2, pair, 0)
+    weave(back(steps - 1, p_b, ds_b))
+    pass_on(steps - 1)
+    swap_out(h)
 
     def out_copy(j, r):
         src, dst = ((out_k, dk_hbm), (out_v, dv_hbm))[j]
@@ -342,10 +407,10 @@
         own = pl.ds(HALF * h, HALF)
 
         def body(b, _):
-            t = pl.multiple_of(b * 32, 32)
-            part = pl.ds(t, 32)
-            accs = pl.ds(pl.multiple_of((r + 1) * WINDOW + t, 32), 32)
-            outs = pl.ds(pl.multiple_of(r * WINDOW + t, 32), 32)
+            t = pl.multiple_of(b * CHUNK, CHUNK)
+            part = pl.ds(t, CHUNK)
+            accs = pl.ds(pl.multiple_of((r + 1) * WINDOW + t, CHUNK), CHUNK)
+            outs = pl.ds(pl.multiple_of(r * WINDOW + t, CHUNK), CHUNK)
             for j, acc, scale, out in ((0, ak, SCALE, out_k), (1, av, None, out_v)):
                 val = acc[own, accs]
                 if scale is not None:
@@ -356,7 +421,7 @@
                 out[outs] = jnp.swapaxes(val.astype(bf16), 0, 1)
             return 0
 
-        lax.fori_loop(0, WINDOW // 32, body, 0)
+        lax.fori_loop(0, WINDOW // CHUNK, body, 0)
         out_copy(0, r).start()
         out_copy(1, r).start()
 
@@ -385,10 +450,11 @@
             edge_copy(n, 0).wait_send()
             edge_copy(n, 1).wait_send()
 
-        dq_copy(n).wait()
         return 0
 
     lax.fori_loop(0, KV, drain, 0)
+    for part in range(2):
+        dq_copy(part).wait()
 
     def drain_x(i, _):
         for r in range(2):
@@ -402,16 +468,23 @@
             out_copy(j, r).wait()
 
 
-def deliver(dq_in, dk_in, dv_in, dq_out, dk_out, dv_out, sem):
-    copies = []
+def deliver(dq_in, dk_in, dv_in, dq_out, dk_out, dv_out, dq_v, dk_v, dv_v, in_sem, out_sem):
+    ways = ((dq_in, dq_v, dq_out), (dk_in, dk_v, dk_out), (dv_in, dv_v, dv_out))
+    moves = []
     for j in range(PIECES):
         rows = pl.ds(j * (TOK // PIECES), TOK // PIECES)
-        for a, (src, dst) in enumerate(((dq_in, dq_out), (dk_in, dk_out), (dv_in, dv_out))):
-            copies.append(pltpu.make_async_copy(src.at[rows], dst.at[rows], sem.at[a, j]))
-    for copy in copies:
-        copy.start()
-    for copy in copies:
-        copy.wait()
+        for a, (src, mid, dst) in enumerate(ways):
+            moves.append((
+                pltpu.make_async_copy(src.at[rows], mid.at[rows], in_sem.at[a, j]),
+                pltpu.make_async_copy(mid.at[rows], dst.at[rows], out_sem.at[a, j]),
+            ))
+    for load, _ in moves:
+        load.start()
+    for load, store in moves:
+        load.wait()
+        store.start()
+    for _, store in moves:
+        store.wait()
 
 
 def on_device(queries, key_heads, value_heads, out_grad, doc_ids):
@@ -421,24 +494,27 @@
     parts = pl.pallas_call(
         kernel,
         out_shape=(
-            jax.ShapeDtypeStruct((TOK, KV, 2, HD), bf16),
+            jax.ShapeDtypeStruct((TOK, 2, KV, HD), bf16),
             jax.ShapeDtypeStruct((TOK, HALF, HD), bf16),
             jax.ShapeDtypeStruct((TOK, HALF, HD), bf16),
         ),
         in_specs=[hbm, hbm, hbm, hbm, vmem],
         out_specs=(hbm, hbm, hbm),
         scratch_shapes=[
-            pltpu.VMEM((KV, TOK, 2, HD), bf16),
-            pltpu.VMEM((KV, TOK, 2, HD), bf16),
+            pltpu.VMEM((2, TOK, KV, HD), bf16),
+            pltpu.VMEM((2, TOK, KV, HD), bf16),
             pltpu.VMEM((TOK, KV, HD), bf16),
             pltpu.VMEM((TOK, KV, HD), bf16),
+            pltpu.VMEM((2 * KV, TOK, HD), bf16),
+            pltpu.VMEM((2 * KV, TOK, HD), bf16),
             pltpu.VMEM((KV, TOK + WINDOW, HD), bf16),
             pltpu.VMEM((KV, TOK + WINDOW, HD), bf16),
             pltpu.VMEM((4, 384, HD), bf16),
             pltpu.VMEM((256, HD), bf16),
             pltpu.VMEM((4, 128), jnp.int32),
             pltpu.VMEM((6, 128, 128), f32),
-            pltpu.VMEM((KV, TOK, 2, HD), bf16),
+            pltpu.VMEM((2 * KV, TOK, HD), bf16),
+            pltpu.VMEM((2, TOK, KV, HD), bf16),
             pltpu.VMEM((KV, TOK + WINDOW, HD), f32),
             pltpu.VMEM((KV, TOK + WINDOW, HD), f32),
             pltpu.VMEM((KV, 2, WINDOW, HD), bf16),
@@ -447,7 +523,15 @@
             pltpu.VMEM((HALF, 2, 2, WINDOW, HD), bf16),
             pltpu.VMEM((TOK, HALF, HD), bf16),
             pltpu.VMEM((TOK, HALF, HD), bf16),
-            dma((2, KV)),
+            pltpu.VMEM((2, 384, 256), f32),
+            pltpu.VMEM((2, 384, 256), f32),
+            pltpu.VMEM((2, 384, 256), f32),
+            pltpu.VMEM((2, 384, 256), f32),
+            pltpu.VMEM((2, 384, 256), bf16),
+            pltpu.VMEM((2, 384, 256), bf16),
+            pltpu.VMEM((2, 384, 256), bf16),
+            pltpu.VMEM((2, 384, 256), bf16),
+            dma((2, 2)),
             dma((2, 2)),
             dma((2, KV)),
             dma((2, KV)),
@@ -457,22 +541,26 @@
             dma((2, KV)),
             dma((HALF, 2, 2)),
             dma((HALF, 2, 2)),
-            dma((KV,)),
+            dma((2,)),
             dma((2, 2)),
         ],
         compiler_params=pltpu.CompilerParams(
             collective_id=0, has_side_effects=True, vmem_limit_bytes=56 * 1024 * 1024
         ),
         cost_estimate=pl.CostEstimate(flops=8 * 10**9, bytes_accessed=9 * 2**20, transcendentals=3 * 10**6),
-    )(queries, key_heads, value_heads, out_grad, doc_ids.reshape(4, 128))
-    return pl.pallas_call(
+    )(
+        queries.reshape(TOK, 2, KV, HD), key_heads, value_heads, out_grad.reshape(TOK, 2, KV, HD),
+        doc_ids.reshape(4, 128),
+    )
+    query_grad, key_grad, value_grad = pl.pallas_call(
         deliver,
         out_shape=tuple(jax.ShapeDtypeStruct(p.shape, p.dtype) for p in parts),
         in_specs=[hbm] * 3,
         out_specs=(hbm,) * 3,
-        scratch_shapes=[dma((3, PIECES))],
+        scratch_shapes=[pltpu.VMEM(p.shape, p.dtype) for p in parts] + [dma((3, PIECES)), dma((3, PIECES))],
         compiler_params=pltpu.CompilerParams(vmem_limit_bytes=56 * 1024 * 1024),
     )(*parts)
+    return query_grad.reshape(TOK, KV, 2, HD), key_grad, value_grad
 
 
 def solution(mesh):

time: 138 us -> 45.7 us (0.33)
  Pallas kernels: 137 us -> 44.6 us
    pallas_call x1, Pallas kernels: 96.5 us -> 2.9 us  [on_device(): pl.pallas_call(deliver, out_shape=tuple((jax.ShapeDtypeStruct(p.shape, p....]
where the time goes in v3:
time: 45.7 us; the launch traced here: 45.3 us
  Pallas kernels  44.6 us (98%)
  between operations  0.64 us (1%)
    pallas_call x1, Pallas kernels, on_device(): pl.pallas_call(kernel, out_shape=(jax.ShapeDtypeStruct((TOK, 2, KV, HD),...  41.7 us
    pallas_call x1, Pallas kernels, on_device(): pl.pallas_call(deliver, out_shape=tuple((jax.ShapeDtypeStruct(p.shape, p....  2.9 us

profile of v3, /device:TPU:25, one launch (start us, length us, event | category | flops | bytes accessed | tf_op | source)
XLA Modules:
  0.0 45.3 jit_solution(7091470482376712547)
XLA Ops:
  0.6 41.7 %shard_map.76 = (bf16[512,2,8,128]{3,2,1,0:T(8,128)(2,1)}, bf16[512,4,128]{2,1,0:T(4,128)(2,1)}, bf16[512,4,128]{2,1,0:T(4,128)(2,1)}) custom-call(bf16[512,2,8,128]{3,2,1,0:T(8,128)(2,1)} %bitcast.4, bf16[512,8,128]{2,1,0:T(8,128)(2,1)} %k_hbm.1, bf16[512,8,128]{2,1,0:T(8,128)(2,1)} %v_hbm.1, bf16[512,2,8,128]{3,2,1,0:T(8,128)(2,1)} %bitcast.5, ...), custom_call_target="tpu_custom_call" | custom-call | flops 8000000000 | bytes 9437184 | tf_op jit(solution)/shard_map/pallas_call | solution.py:494
  42.4 2.9 %shard_map.77 = (bf16[512,2,8,128]{3,2,1,0:T(8,128)(2,1)}, bf16[512,4,128]{2,1,0:T(4,128)(2,1)}, bf16[512,4,128]{2,1,0:T(4,128)(2,1)}) custom-call(bf16[512,2,8,128]{3,2,1,0:T(8,128)(2,1)} %get-tuple-element.9.dq_in, bf16[512,4,128]{2,1,0:T(4,128)(2,1)} %get-tuple-element.10.dk_in, bf16[512,4,128]{2,1,0:T(4,128)(2,1)} %get-tuple-element.11.dv_in), custom_call_target="tpu_custom_call" | custom-call | tf_op jit(solution)/shard_map/pallas_call | solution.py:555

commit v4 on v3

--- a/solution.py
+++ b/solution.py
@@ -18,7 +18,7 @@
 SCALE = HD**-0.5
 EXP_SCALE = SCALE * 1.4426950408889634
 HIDDEN = -1e30
-PIECES = 4
+PIECES = 2
 CHUNK = 128
 NT = (((1,), (1,)), ((), ()))
 NN = (((1,), (0,)), ((), ()))
@@ -150,17 +150,22 @@
     def _():
         pl.semaphore_wait(barrier, 2)
 
+    def send_halo(grp):
+        @pl.when(has_next)
+        def _():
+            def body(i, _):
+                n = head_of(grp, i)
+                halo_copy(n, 0).start()
+                halo_copy(jnp.where(before_turn, lax.rem(n + HALF, KV), n), 1).start()
+                return 0
+
+            lax.fori_loop(0, HALF, body, 0)
+
     @pl.when(has_next)
     def _():
         doc_copy().start()
 
-        def send_halo(i, _):
-            n = head_of(i // HALF, lax.rem(i, HALF))
-            halo_copy(n, 0).start()
-            halo_copy(jnp.where(before_turn, lax.rem(n + HALF, KV), n), 1).start()
-            return 0
-
-        lax.fori_loop(0, KV, send_halo, 0)
+    send_halo(0)
 
     for j, src, dst in ((0, k_raw, kt), (1, v_raw, vt)):
         kv_copy(j, 0).wait()
@@ -182,17 +187,17 @@
     build_mask(2)
     build_mask(3)
 
-    def edge_copy(n, j):
+    def edge_copy(n):
         cross = after_turn & (n // HALF != h)
         slot = jnp.where(cross, lax.rem(n + HALF, KV), n)
         dev = (c - 1, jnp.where(cross, 1 - h, h))
-        return remote(edge_s.at[n, j], edge_r.at[slot, j], e_send.at[j, n], e_recv.at[j, slot], dev)
-
-    def edge_arrival(n, j):
-        return remote(edge_s.at[n, j], edge_r.at[n, j], e_send.at[j, n], e_recv.at[j, n], prv)
-
-    def x_copy(i, r, j):
-        return remote(xs.at[i, r, j], xr.at[i, r, j], x_send.at[i, r, j], x_recv.at[i, r, j], partner)
+        return remote(edge_s.at[n], edge_r.at[slot], e_send.at[n], e_recv.at[slot], dev)
+
+    def edge_arrival(n):
+        return remote(edge_s.at[n], edge_r.at[n], e_send.at[n], e_recv.at[n], prv)
+
+    def x_copy(i, r):
+        return remote(xs.at[i, r], xr.at[i, r], x_send.at[i, r], x_recv.at[i, r], partner)
 
     def dq_copy(part):
         return pltpu.make_async_copy(dq_s.at[part], dq_hbm.at[:, part], dq_sem.at[part])
@@ -229,14 +234,12 @@
         def _():
             @pl.when(has_next)
             def _():
-                edge_arrival(n, 0).wait_recv()
-                edge_arrival(n, 1).wait_recv()
+                edge_arrival(n).wait_recv()
 
             xs[i, 1, 0] = (ak[n, TOK:] * SCALE + edge_r[n, 0].astype(f32)).astype(bf16)
             xs[i, 1, 1] = (av[n, TOK:] + edge_r[n, 1].astype(f32)).astype(bf16)
 
-        x_copy(i, 1, 0).start()
-        x_copy(i, 1, 1).start()
+        x_copy(i, 1).start()
 
     def plan(s):
         i = lax.rem(s, HALF)
@@ -323,19 +326,17 @@
         def _():
             edge_s[n, 0] = (ak[n, :WINDOW] * SCALE).astype(bf16)
             edge_s[n, 1] = av[n, :WINDOW].astype(bf16)
-            edge_copy(n, 0).start()
-            edge_copy(n, 1).start()
+            edge_copy(n).start()
 
         @pl.when((late == 1) & (grp == 0))
         def _():
             xs[i, 0, 0] = (ak[n, WINDOW:TOK] * SCALE).astype(bf16)
             xs[i, 0, 1] = av[n, WINDOW:TOK].astype(bf16)
-            x_copy(i, 0, 0).start()
-            x_copy(i, 0, 1).start()
-
-        @pl.when((par == 0) & (s >= 1) & (s <= HALF))
-        def _():
-            send_tail_sums(s - 1)
+            x_copy(i, 0).start()
+
+        @pl.when((par == 0) & (s < HALF))
+        def _():
+            send_tail_sums(s)
 
         @pl.when((par == 1) & (s >= 2 * HALF) & (s < 3 * HALF))
         def _():
@@ -350,6 +351,7 @@
     swap_in(1 - h)
     prepare(0)
     weave(front(0, s_a, dp_a))
+    send_halo(1)
 
     def pair(at, _):
         for k in range(2):
@@ -384,20 +386,17 @@
 
     def finish(r):
         def wait_head(i, _):
-            x_copy(i, r, 0).wait_recv()
-            x_copy(i, r, 1).wait_recv()
+            x_copy(i, r).wait_recv()
             if r == 1:
 
                 @pl.when(has_next)
                 def _():
-                    edge_arrival(HALF * h + i, 0).wait_recv()
-                    edge_arrival(HALF * h + i, 1).wait_recv()
+                    edge_arrival(HALF * h + i).wait_recv()
 
                 @pl.when(before_turn)
                 def _():
                     n, slot = head_of(1, i), head_of(0, i)
-                    edge_arrival(slot, 0).wait_recv()
-                    edge_arrival(slot, 1).wait_recv()
+                    edge_arrival(slot).wait_recv()
                     ak[n, TOK:] += edge_r[slot, 0].astype(f32) * (1.0 / SCALE)
                     av[n, TOK:] += edge_r[slot, 1].astype(f32)
 
@@ -447,8 +446,7 @@
 
         @pl.when(has_prev)
         def _():
-            edge_copy(n, 0).wait_send()
-            edge_copy(n, 1).wait_send()
+            edge_copy(n).wait_send()
 
         return 0
 
@@ -458,8 +456,7 @@
 
     def drain_x(i, _):
         for r in range(2):
-            for j in range(2):
-                x_copy(i, r, j).wait_send()
+            x_copy(i, r).wait_send()
         return 0
 
     lax.fori_loop(0, HALF, drain_x, 0)
@@ -537,10 +534,10 @@
             dma((2, KV)),
             dma(()),
             dma(()),
-            dma((2, KV)),
-            dma((2, KV)),
-            dma((HALF, 2, 2)),
-            dma((HALF, 2, 2)),
+            dma((KV,)),
+            dma((KV,)),
+            dma((HALF, 2)),
+            dma((HALF, 2)),
             dma((2,)),
             dma((2, 2)),
         ],

time: 45.7 us -> 45.4 us (level)
  no operation moved by 1% of the time
where the time goes in v4:
time: 45.4 us; the launch traced here: 45 us
  Pallas kernels  44.4 us (98%)
  between operations  0.64 us (1%)
    pallas_call x1, Pallas kernels, on_device(): pl.pallas_call(kernel, out_shape=(jax.ShapeDtypeStruct((TOK, 2, KV, HD),...  41.4 us
    pallas_call x1, Pallas kernels, on_device(): pl.pallas_call(deliver, out_shape=tuple((jax.ShapeDtypeStruct(p.shape, p....  2.98 us

profile of v4, /device:TPU:25, one launch (start us, length us, event | category | flops | bytes accessed | tf_op | source)
XLA Modules:
  0.0 45.0 jit_solution(4650122714961584673)
XLA Ops:
  0.6 41.4 %shard_map.76 = (bf16[512,2,8,128]{3,2,1,0:T(8,128)(2,1)}, bf16[512,4,128]{2,1,0:T(4,128)(2,1)}, bf16[512,4,128]{2,1,0:T(4,128)(2,1)}) custom-call(bf16[512,2,8,128]{3,2,1,0:T(8,128)(2,1)} %bitcast.4, bf16[512,8,128]{2,1,0:T(8,128)(2,1)} %k_hbm.1, bf16[512,8,128]{2,1,0:T(8,128)(2,1)} %v_hbm.1, bf16[512,2,8,128]{3,2,1,0:T(8,128)(2,1)} %bitcast.5, ...), custom_call_target="tpu_custom_call" | custom-call | flops 8000000000 | bytes 9437184 | tf_op jit(solution)/shard_map/pallas_call | solution.py:491
  42.1 3.0 %shard_map.77 = (bf16[512,2,8,128]{3,2,1,0:T(8,128)(2,1)}, bf16[512,4,128]{2,1,0:T(4,128)(2,1)}, bf16[512,4,128]{2,1,0:T(4,128)(2,1)}) custom-call(bf16[512,2,8,128]{3,2,1,0:T(8,128)(2,1)} %get-tuple-element.9.dq_in, bf16[512,4,128]{2,1,0:T(4,128)(2,1)} %get-tuple-element.10.dk_in, bf16[512,4,128]{2,1,0:T(4,128)(2,1)} %get-tuple-element.11.dv_in), custom_call_target="tpu_custom_call" | custom-call | tf_op jit(solution)/shard_map/pallas_call | solution.py:552

commit v5 on v4

--- a/solution.py
+++ b/solution.py
@@ -88,6 +88,27 @@
         for j in (0, 1):
             qg_copy(j, part).start()
 
+    key_row = lax.broadcasted_iota(jnp.int32, (128, 128), 0)
+    tok_col = lax.broadcasted_iota(jnp.int32, (128, 128), 1)
+    onehot[:128] = jnp.where(key_row == tok_col, 1.0, 0.0).astype(bf16)
+    onehot[128:] = jnp.where(key_row == tok_col, 1.0, 0.0).astype(bf16)
+
+    def doc_columns(block, ref, r):
+        wide = jnp.broadcast_to(ref[r : r + 1, :], (128, 128)).astype(f32)
+        doc_col[block] = wide.T
+
+    def build_mask(t):
+        docs = jnp.broadcast_to(doc_ref[t : t + 1, :], (128, 128)).astype(f32)
+        for b, inside in enumerate((key_row > tok_col, None, key_row <= tok_col)):
+            same = doc_col[t + b] == docs
+            seen = same if inside is None else same & inside
+            mask[t, b * 128 : (b + 1) * 128] = jnp.where(seen, 0.0, HIDDEN).astype(bf16)
+
+    for b in range(4):
+        doc_columns(2 + b, doc_ref, b)
+    build_mask(2)
+    build_mask(3)
+
     def clear(n, _):
         ak[n] = jnp.zeros((TOK + WINDOW, HD), f32)
         av[n] = jnp.zeros((TOK + WINDOW, HD), f32)
@@ -95,12 +116,6 @@
 
     lax.fori_loop(0, KV, clear, 0)
 
-    key_row = lax.broadcasted_iota(jnp.int32, (128, 128), 0)
-    tok_col = lax.broadcasted_iota(jnp.int32, (128, 128), 1)
-    onehot[:128] = jnp.where(key_row == tok_col, 1.0, 0.0).astype(bf16)
-    onehot[128:] = jnp.where(key_row == tok_col, 1.0, 0.0).astype(bf16)
-    p_b[...] = jnp.zeros(p_b.shape, bf16)
-    ds_b[...] = jnp.zeros(ds_b.shape, bf16)
 
     @pl.when(first)
     def _():
@@ -170,22 +185,6 @@
     for j, src, dst in ((0, k_raw, kt), (1, v_raw, vt)):
         kv_copy(j, 0).wait()
         swap(src, dst, 0)
-
-    def doc_columns(block, ref, r):
-        wide = jnp.broadcast_to(ref[r : r + 1, :], (128, 128)).astype(f32)
-        doc_col[block] = wide.T
-
-    def build_mask(t):
-        docs = jnp.broadcast_to(doc_ref[t : t + 1, :], (128, 128)).astype(f32)
-        for b, inside in enumerate((key_row > tok_col, None, key_row <= tok_col)):
-            same = doc_col[t + b] == docs
-            seen = same if inside is None else same & inside
-            mask[t, b * 128 : (b + 1) * 128] = jnp.where(seen, 0.0, HIDDEN).astype(bf16)
-
-    for b in range(4):
-        doc_columns(2 + b, doc_ref, b)
-    build_mask(2)
-    build_mask(3)
 
     def edge_copy(n):
         cross = after_turn & (n // HALF != h)
@@ -353,28 +352,21 @@
     weave(front(0, s_a, dp_a))
     send_halo(1)
 
+    prepare(1)
+    weave(middle(*slots[0]), front(1, s_b, dp_b))
+
     def pair(at, _):
         for k in range(2):
-            s = 2 * at + k
-            here, other = slots[k], slots[1 - k]
-
-            @pl.when(s + 1 < steps)
-            def _():
-                prepare(s + 1)
-
-            weave(
-                middle(*here),
-                back(jnp.maximum(s - 1, 0), other[2], other[3]),
-                front(jnp.minimum(s + 1, steps - 1), other[0], other[1]),
-            )
-
-            @pl.when(s >= 1)
-            def _():
-                pass_on(s - 1)
-
+            s = 2 * at + k + 1
+            here, other = slots[1 - k], slots[k]
+            prepare(s + 1)
+            weave(middle(*here), back(s - 1, other[2], other[3]), front(s + 1, other[0], other[1]))
+            pass_on(s - 1)
         return 0
 
-    lax.fori_loop(0, steps // 2, pair, 0)
+    lax.fori_loop(0, steps // 2 - 1, pair, 0)
+    weave(middle(*slots[1]), back(steps - 2, p_a, ds_a))
+    pass_on(steps - 2)
     weave(back(steps - 1, p_b, ds_b))
     pass_on(steps - 1)
     swap_out(h)

time: 45.4 us -> 45.2 us (level)
  no operation moved by 1% of the time
where the time goes in v5:
time: 45.2 us; the launch traced here: 45 us
  Pallas kernels  44.4 us (98%)
  between operations  0.64 us (1%)
    pallas_call x1, Pallas kernels, on_device(): pl.pallas_call(kernel, out_shape=(jax.ShapeDtypeStruct((TOK, 2, KV, HD),...  41.4 us
    pallas_call x1, Pallas kernels, on_device(): pl.pallas_call(deliver, out_shape=tuple((jax.ShapeDtypeStruct(p.shape, p....  2.98 us

profile of v5, /device:TPU:25, one launch (start us, length us, event | category | flops | bytes accessed | tf_op | source)
XLA Modules:
  0.0 45.0 jit_solution(16064179564507343825)
XLA Ops:
  0.6 41.4 %shard_map.76 = (bf16[512,2,8,128]{3,2,1,0:T(8,128)(2,1)}, bf16[512,4,128]{2,1,0:T(4,128)(2,1)}, bf16[512,4,128]{2,1,0:T(4,128)(2,1)}) custom-call(bf16[512,2,8,128]{3,2,1,0:T(8,128)(2,1)} %bitcast.4, bf16[512,8,128]{2,1,0:T(8,128)(2,1)} %k_hbm.1, bf16[512,8,128]{2,1,0:T(8,128)(2,1)} %v_hbm.1, bf16[512,2,8,128]{3,2,1,0:T(8,128)(2,1)} %bitcast.5, ...), custom_call_target="tpu_custom_call" | custom-call | flops 8000000000 | bytes 9437184 | tf_op jit(solution)/shard_map/pallas_call | solution.py:483
  42.1 3.0 %shard_map.77 = (bf16[512,2,8,128]{3,2,1,0:T(8,128)(2,1)}, bf16[512,4,128]{2,1,0:T(4,128)(2,1)}, bf16[512,4,128]{2,1,0:T(4,128)(2,1)}) custom-call(bf16[512,2,8,128]{3,2,1,0:T(8,128)(2,1)} %get-tuple-element.9.dq_in, bf16[512,4,128]{2,1,0:T(4,128)(2,1)} %get-tuple-element.10.dk_in, bf16[512,4,128]{2,1,0:T(4,128)(2,1)} %get-tuple-element.11.dv_in), custom_call_target="tpu_custom_call" | custom-call | tf_op jit(solution)/shard_map/pallas_call | solution.py:544
